TPU v7x, 32 devices: a whole 2x2x4 slice. The times are simulated.
32 devices in a mesh: sec: 8 (over z, y), dev: 4 (over x, core).
Axes of the slice: x: 2, y: 2, z: 4, core: 2. Of those that a mesh axis runs over, the one named last changes fastest.
Arguments:
- latents: float32 [8, 4, 128, 128], P('sec', None, 'dev'), may hold values from -6 to 6
- noise: float32 [6, 8, 4, 128, 128], P(None, 'sec', None, 'dev'), may hold values from -6 to 6
- rewards: float32 [8], P('sec'), may hold values from -12 to 12
- prompt_ids: int32 [8], P('sec'), may hold values from 0 to 3
- context: bfloat16 [4, 77, 2048], replicated, may hold values from -6 to 6
- time_bias: float32 [6, 640], replicated, may hold values from -6 to 6
- gain_first: float32 [640], replicated, may hold values from 0.25 to 1.75
- gain_second: float32 [640], replicated, may hold values from 0.25 to 1.75
- gain_third: float32 [640], replicated, may hold values from 0.25 to 1.75
- w_in: bfloat16 [16, 640], P('sec', 'dev'), may hold values from -1.5 to 1.5
- w_conv: bfloat16 [5760, 640], P('sec', 'dev'), may hold values from -0.078125 to 0.078125
- w_query: bfloat16 [640, 640], P('sec', 'dev'), may hold values from -0.25 to 0.25
- w_key: bfloat16 [2048, 640], P('sec', 'dev'), may hold values from -0.125 to 0.125
- w_value: bfloat16 [2048, 640], P('sec', 'dev'), may hold values from -0.125 to 0.125
- w_attn_out: bfloat16 [640, 640], P('sec', 'dev'), may hold values from -0.25 to 0.25
- w_final: float32 [640, 16], P('sec', 'dev'), may hold values from -0.25 to 0.25
- moment_first: float32 [640, 16], P('sec', 'dev'), may hold values from -6 to 6
- moment_second: float32 [640, 16], P('sec', 'dev'), may hold values from 0.05 to 5
Outputs:
- final_latents: float32 [8, 4, 128, 128], P('sec', None, 'dev')
- new_final_weight: float32 [640, 16], P('sec', 'dev')
- moment_one: float32 [640, 16], P('sec', 'dev')
- moment_two: float32 [640, 16], P('sec', 'dev')
All inputs are finite; a program needn't handle non-finite values.
Results may differ from a plain program's by a relative error of at most 0.0075.
Values may be sent and summed in bfloat16 or wider, within the bound.
No kernel may reach another device: no remote copies, remote signals or barrier semaphores. Data moves between devices by JAX's collectives and lax.ppermute only.
A program may use at most 128 MiB of HBM per device.

v0:
```python
import functools
import math

import jax
import jax.numpy as jnp
from jax import lax
from jax.experimental import pallas as pl
from jax.experimental.pallas import tpu as pltpu
from jax.sharding import PartitionSpec as P

HEAD = 64
STEPS = 6
GROUP = 3
HALO = 4
CHUNK_ROWS = 4

alpha_bars = (0.1, 0.15, 0.21, 0.28, 0.36, 0.45, 0.55)
norm_eps = 1e-06
learn_rate = 0.001


def plan(step_index):
    current = alpha_bars[step_index]
    following = alpha_bars[step_index + 1]
    sigma = math.sqrt((1.0 - following) / (1.0 - current)) * math.sqrt(1.0 - current / following)
    scale = math.sqrt(following / current)
    beta = math.sqrt(1.0 - following - sigma * sigma) - scale * math.sqrt(1.0 - current)
    return (scale, beta, sigma)


def swap(value, axis, mask):
    size = lax.axis_size(axis)
    return lax.ppermute(value, axis, [(i, i ^ mask) for i in range(size)])


def bit_of(axis, mask):
    return (lax.axis_index(axis) & mask) != 0


def doubled_gather(value, axis):
    mask = 1
    while mask < lax.axis_size(axis):
        other = swap(value, axis, mask)
        upper = bit_of(axis, mask)
        value = jnp.concatenate(
            [jnp.where(upper, other, value), jnp.where(upper, value, other)], axis=0
        )
        mask *= 2
    return value


def halved_sum(value, axis, link=jnp.float32):
    mask = lax.axis_size(axis) // 2
    while mask >= 1:
        half = value.shape[0] // 2
        upper = bit_of(axis, mask)
        kept = jnp.where(upper, value[half:], value[:half])
        sent = jnp.where(upper, value[:half], value[half:])
        value = kept + swap(sent.astype(link), axis, mask).astype(value.dtype)
        mask //= 2
    return value


def with_halo(shard, axis, dim, width):
    size, length = (lax.axis_size(axis), shard.shape[dim])
    up = [(i, i + 1) for i in range(size - 1)]
    down = [(j, i) for i, j in up]
    last = lax.slice_in_dim(shard, length - width, length, axis=dim)
    first = lax.slice_in_dim(shard, 0, width, axis=dim)
    before = lax.ppermute(last, axis, up)
    after = lax.ppermute(first, axis, down)
    return jnp.concatenate([before, shard, after], axis=dim)


def lane_order(breadth):
    half = breadth // 2
    lane = jnp.arange(breadth)
    return (lane[:, None] == (2 * (lane % half) + lane // half)[None, :]).astype(jnp.float32)


def to_tokens(latent):
    count, chans, height, breadth = latent.shape
    split = jnp.dot(latent, lane_order(breadth), precision=lax.Precision.HIGHEST)
    blocks = split.reshape(count, chans, height // 2, 2, 2, breadth // 2)
    return blocks.transpose(0, 1, 3, 4, 2, 5).reshape(
        count, chans * 4, height * breadth // 4
    )


def from_tokens(tokens, rows, cols):
    feats = tokens.shape[0]
    blocks = tokens.reshape(feats // 4, 2, 2, rows, cols).transpose(0, 3, 1, 2, 4)
    return jnp.dot(
        blocks.reshape(feats // 4, 2 * rows, 2 * cols),
        lane_order(2 * cols).T,
        precision=lax.Precision.HIGHEST,
    )


def rms_scale(values, gain):
    mean_square = jnp.mean(values * values, axis=-1, keepdims=True)
    return values * lax.rsqrt(mean_square + norm_eps) * gain


def silu(values):
    return 0.5 * values * (1.0 + jnp.tanh(0.5 * values))


def steps_kernel(
    rows,
    cols,
    counts,
    flags,
    factors,
    packed,
    x_in,
    noise,
    key_blocks,
    value_blocks,
    bias,
    gains,
    w_in,
    w_final,
    x_out,
    grad_out,
    w_conv,
    w_query,
    w_attn,
    hidden,
    columns,
    state,
    sems,
):
    group = bias.shape[0]
    feats, chans = w_in.shape
    parts = packed.shape[0]
    copies = []
    offset = 0
    for which, (count, ref) in enumerate(zip(counts, (w_conv, w_query, w_attn))):
        copies.append([])
        for part in range(parts):
            copy = pltpu.make_async_copy(
                packed.at[part, pl.ds(offset, count)],
                ref.at[pl.ds(part * count, count)],
                sems.at[which, part],
            )
            copy.start()
            copies[-1].append(copy)
        offset += count
    state[...] = x_in[...]
    grad_out[...] = jnp.zeros_like(grad_out)
    pairs = key_blocks.shape[0]
    wide = 2 * HEAD
    size = CHUNK_ROWS * cols
    token = lax.broadcasted_iota(jnp.int32, (size, 1), 0)
    lane_token = lax.broadcasted_iota(jnp.int32, (1, size), 1)
    col = lax.rem(token, cols)

    def activate(step, chunk):
        start = pl.multiple_of(chunk * size, size)
        span = pl.ds(start, size)
        before_norm = (
            lax.dot_general(
                state[:, span].astype(jnp.bfloat16),
                w_in[...],
                (((0,), (0,)), ((), ())),
                preferred_element_type=jnp.float32,
            )
            + bias[pl.ds(step, 1), :]
        )
        hidden[span, :] = before_norm
        act = silu(rms_scale(before_norm, gains[0:1, :]))
        inside = jnp.where(
            start + token < HALO * cols,
            flags[0],
            jnp.where(start + token >= (HALO + rows) * cols, flags[1], 1.0),
        )
        act = act * inside
        left = jnp.where(col == 0, 0.0, pltpu.roll(act, 1, 0))
        right = jnp.where(col == cols - 1, 0.0, pltpu.roll(act, size - 1, 0))
        columns[span, 0:chans] = left.astype(jnp.bfloat16)
        columns[span, chans : 2 * chans] = act.astype(jnp.bfloat16)
        columns[span, 2 * chans : 3 * chans] = right.astype(jnp.bfloat16)

    def convolve(start):
        mixed = hidden[pl.ds(start, size), :]
        for dr in range(3):
            mixed = mixed + jnp.dot(
                columns[pl.ds(start + (dr - 1) * cols, size), :],
                w_conv[dr * 3 * chans : (dr + 1) * 3 * chans, :],
                preferred_element_type=jnp.float32,
            )
        return mixed

    def finish(step, start, mixed):
        normed = rms_scale(mixed, gains[1:2, :]).astype(jnp.bfloat16)
        queries = jnp.dot(normed, w_query[...], preferred_element_type=jnp.float32).astype(
            jnp.bfloat16
        )
        heads = []
        for pair in range(pairs):
            scores = jnp.dot(
                queries[:, pair * wide : (pair + 1) * wide],
                key_blocks[pair],
                preferred_element_type=jnp.float32,
            )
            sums = jnp.dot(
                jnp.exp(scores).astype(jnp.bfloat16),
                value_blocks[pair],
                preferred_element_type=jnp.float32,
            )
            heads.append((sums[:, :wide] / sums[:, wide:]).astype(jnp.bfloat16))
        attended = jnp.concatenate(heads, axis=1)
        output = mixed + jnp.dot(attended, w_attn[...], preferred_element_type=jnp.float32)
        act = silu(rms_scale(output, gains[2:3, :])).astype(jnp.bfloat16)
        predicted = jnp.dot(act, w_final[...], preferred_element_type=jnp.float32)
        span = pl.ds(start, size)
        noise_now = noise[step, :, span]
        state[:, span] = (
            factors[step, 0] * state[:, span]
            + factors[step, 1] * predicted.T
            + factors[step, 2] * noise_now
        )
        place = start + lane_token
        own = (place >= HALO * cols) & (place < (HALO + rows) * cols)
        weights = jnp.where(own, noise_now, 0.0)
        upper = weights.astype(jnp.bfloat16)
        lower = (weights - upper.astype(jnp.float32)).astype(jnp.bfloat16)
        share = jnp.dot(
            jnp.concatenate([upper, lower], axis=0), act, preferred_element_type=jnp.float32
        )
        grad_out[...] += factors[step, 3] * (share[:feats] + share[feats:])

    chunks = state.shape[1] // size

    def one_step(step, carry):
        def fill(chunk, carry):
            activate(step, chunk)
            return carry

        lax.fori_loop(0, chunks, fill, 0)
        last = step == group - 1
        base = jnp.where(last, HALO, HALO // 2) * cols
        count = jnp.where(last, chunks - 2, chunks - 1)

        @pl.when(step == 0)
        def _():
            for some in copies:
                for copy in some:
                    copy.wait()

        def place(number):
            return pl.multiple_of(base + number * size, 2 * cols)

        def body(number, mixed):
            following = convolve(place(number))
            finish(step, place(number - 1), mixed)
            return following

        mixed = lax.fori_loop(1, count, body, convolve(place(0)))
        finish(step, place(count - 1), mixed)
        return carry

    lax.fori_loop(0, group, one_step, 0)
    x_out[...] = state[:, HALO * cols : (HALO + rows) * cols]


def run_steps(rows, cols, counts, flags, factors, packed, x, noise, rest, bias):
    key_blocks, value_blocks, gains, w_in, w_final = rest
    feats, chans = w_in.shape
    parts = packed.shape[0]
    tall = (rows + 2 * HALO) * cols
    vmem = pl.BlockSpec(memory_space=pltpu.VMEM)
    smem = pl.BlockSpec(memory_space=pltpu.SMEM)
    token_rows = sum(rows + 2 * k for k in range(GROUP)) * cols
    return pl.pallas_call(
        functools.partial(steps_kernel, rows, cols, counts),
        out_shape=(
            jax.ShapeDtypeStruct((feats, rows * cols), jnp.float32),
            jax.ShapeDtypeStruct((feats, chans), jnp.float32),
        ),
        in_specs=[smem, smem, pl.BlockSpec(memory_space=pl.ANY)] + [vmem] * 8,
        out_specs=(vmem, vmem),
        scratch_shapes=[
            pltpu.VMEM((9 * chans, chans), jnp.bfloat16),
            pltpu.VMEM((chans, chans), jnp.bfloat16),
            pltpu.VMEM((chans, chans), jnp.bfloat16),
            pltpu.VMEM((tall, chans), jnp.float32),
            pltpu.VMEM((tall, 3 * chans), jnp.bfloat16),
            pltpu.VMEM((feats, tall), jnp.float32),
            pltpu.SemaphoreType.DMA((3, parts)),
        ],
        compiler_params=pltpu.CompilerParams(vmem_limit_bytes=48 * 2**20),
        cost_estimate=pl.CostEstimate(
            flops=2 * token_rows * chans * chans * 12,
            bytes_accessed=12 * chans * chans * 2,
            transcendentals=4 * token_rows * chans,
        ),
    )(flags, factors, packed, x, noise, key_blocks, value_blocks, bias, gains, w_in, w_final)


def advantages(onehot, own, rewards, own_reward):
    counts = jnp.sum(onehot, axis=0)
    sums = jnp.sum(onehot * rewards[:, None], axis=0)
    squares = jnp.sum(onehot * (rewards * rewards)[:, None], axis=0)
    safe_count = jnp.maximum(counts, 1.0)
    means = sums / safe_count
    spreads = jnp.sqrt(jnp.maximum(squares / safe_count - means * means, 1.0))
    own_mean = jnp.sum(own * means)
    own_spread = jnp.sum(own * spreads)
    return (own_reward - own_mean) / own_spread


def per_device(
    latents,
    noise,
    rewards,
    prompt_ids,
    context,
    time_bias,
    gain_first,
    gain_second,
    gain_third,
    w_in,
    w_conv,
    w_query,
    w_key,
    w_value,
    w_attn_out,
    w_final,
    moment_first,
    moment_second,
):
    sec_count = lax.axis_size("sec")
    dev_count = lax.axis_size("dev")
    prompt_count, context_tokens, _ = context.shape
    assert latents.shape[0] == 1
    col_piece = w_conv.shape[1]
    chans = col_piece * dev_count
    feats = w_in.shape[0] * sec_count
    rows, cols = latents.shape[2] // 2, latents.shape[3] // 2

    pieces = [
        w_conv,
        w_query,
        w_attn_out,
        w_in,
        w_final.astype(jnp.bfloat16).reshape(-1, col_piece),
    ]
    counts = [piece.shape[0] for piece in pieces]
    used = sum(counts)
    unit = 16 * dev_count
    padded = -(-used // unit) * unit
    pieces.append(jnp.zeros((padded - used, col_piece), jnp.bfloat16))
    block = jnp.concatenate(pieces, axis=0)
    block = lax.all_to_all(block, "dev", split_axis=0, concat_axis=1, tiled=True)
    packed = lax.all_gather(block, ("sec", "dev"), axis=0, tiled=True)
    packed = packed.reshape(sec_count, padded, chans)
    at = counts[0] + counts[1] + counts[2]
    in_full = packed[:, at : at + counts[3]].reshape(feats, chans)
    at += counts[3]
    final_full = (
        packed[:, at : at + counts[4]]
        .reshape(sec_count, counts[4], dev_count, col_piece)
        .transpose(0, 2, 1, 3)
        .reshape(sec_count, dev_count, chans // sec_count, feats // dev_count)
        .transpose(0, 2, 1, 3)
        .reshape(chans, feats)
    )
    big = counts[:3]
    if any(count % 16 for count in big):
        packed = jnp.concatenate(
            [
                packed[:, sum(big[:k]) : sum(big[: k + 1])].reshape(-1, chans)
                for k in range(3)
            ],
            axis=0,
        )[None]
        big = [count * sec_count for count in big]

    both = jnp.stack([rewards, prompt_ids.astype(jnp.float32)], axis=1)
    both = doubled_gather(both, "sec")
    all_rewards = both[:, 0]
    catalog = jnp.arange(prompt_count, dtype=jnp.int32)
    onehot = (both[:, 1].astype(jnp.int32)[:, None] == catalog[None, :]).astype(jnp.float32)
    own = (prompt_ids == catalog).astype(jnp.float32)
    advantage = advantages(onehot, own, all_rewards, rewards[0])

    key_rows = w_key.shape[0]
    tokens_up = -(-context_tokens // 16) * 16
    own_context = lax.dynamic_slice_in_dim(
        context, lax.axis_index("sec") * key_rows, key_rows, axis=2
    )
    own_context = jnp.pad(own_context, ((0, 0), (0, tokens_up - context_tokens), (0, 0)))
    partial = jnp.dot(
        own_context.reshape(prompt_count * tokens_up, key_rows),
        jnp.concatenate([w_key, w_value], axis=1),
        preferred_element_type=jnp.float32,
    ).reshape(prompt_count, tokens_up, 2 * col_piece)
    wanted = jnp.einsum(
        "ip,ptc->itc", onehot, partial, precision=lax.Precision.HIGHEST
    )
    own_part = halved_sum(wanted, "sec", jnp.bfloat16).astype(jnp.bfloat16)
    whole = doubled_gather(own_part, "dev").reshape(dev_count, tokens_up, 2, col_piece)
    whole = whole.transpose(2, 1, 0, 3).reshape(2, tokens_up, chans)
    lane = 2 * HEAD
    pairs = chans // lane
    valid = jnp.arange(tokens_up)[None, :, None] < context_tokens
    by_pair = jnp.where(valid, whole, 0).reshape(2, tokens_up, pairs, 2, HEAD)
    by_pair = jnp.pad(by_pair, ((0, 0), (0, lane - tokens_up), (0, 0), (0, 0), (0, 0)))
    eye = jnp.eye(2, dtype=jnp.bfloat16)
    key_blocks = (
        (by_pair[0] * (1.0 / math.sqrt(HEAD))).astype(jnp.bfloat16).transpose(1, 2, 3, 0)[
            :, :, :, None, :
        ]
        * eye[None, :, None, :, None]
    ).reshape(pairs, lane, 2 * lane)
    value_blocks = (
        by_pair[1].transpose(1, 2, 0, 3)[:, :, :, None, :] * eye[None, :, None, :, None]
    ).reshape(pairs, 2 * lane, lane)
    inside = (jnp.arange(lane) < context_tokens).astype(jnp.bfloat16)
    ones = jnp.broadcast_to(
        inside[None, :, None, None] * eye[:, None, :, None], (2, lane, 2, HEAD)
    ).reshape(1, 2 * lane, lane)
    value_blocks = jnp.concatenate(
        [value_blocks, jnp.broadcast_to(ones, value_blocks.shape)], axis=2
    )

    position = lax.axis_index("dev")
    flags = jnp.stack([position > 0, position < dev_count - 1]).astype(jnp.float32)
    planes = jnp.concatenate([latents, noise[:, 0]], axis=0)
    planes = to_tokens(with_halo(planes, "dev", 2, 2 * HALO))
    x, noise_wide = planes[0], planes[1:]
    plans = [plan(k) for k in range(STEPS)]
    factors = jnp.array([(s, b, g, b / g) for s, b, g in plans], jnp.float32)

    gains = jnp.stack([gain_first, gain_second, gain_third])
    rest = (key_blocks, value_blocks, gains, in_full, final_full)
    gradient = jnp.zeros((feats, chans), jnp.float32)
    for first in range(0, STEPS, GROUP):
        if first:
            x = with_halo(x, "dev", 1, HALO * cols)
        part = slice(first, first + GROUP)
        x, share = run_steps(
            rows,
            cols,
            big,
            flags,
            factors[part],
            packed,
            x,
            noise_wide[part],
            rest,
            time_bias[part],
        )
        gradient = gradient + share
    latent = from_tokens(x, rows, cols)[None]

    gradient = gradient * advantage
    row_piece = chans // sec_count
    arranged = gradient.reshape(dev_count, feats // dev_count, sec_count, row_piece)
    arranged = arranged.transpose(2, 0, 1, 3)
    grad_shard = halved_sum(halved_sum(arranged, "sec")[0], "dev")[0].T
    grad_shard = -grad_shard / sec_count
    moment_one = 0.9 * moment_first + 0.1 * grad_shard
    moment_two = 0.999 * moment_second + 0.001 * grad_shard * grad_shard
    new_weight = w_final - learn_rate * moment_one / (jnp.sqrt(moment_two) + 1e-08)
    return (latent, new_weight, moment_one, moment_two)


def solution(mesh):
    weight = P("sec", "dev")
    placed = (
        (P("sec", None, "dev", None), P(None, "sec", None, "dev", None), P("sec"), P("sec"))
        + (P(),) * 5
        + (weight,) * 9
    )
    return jax.shard_map(
        per_device,
        mesh=mesh,
        in_specs=placed,
        out_specs=(P("sec", None, "dev", None), weight, weight, weight),
        check_vma=False,
    )
```

profile of v0, /device:TPU:0, one launch (start us, length us, event | category | flops | bytes accessed | tf_op | source)
XLA Modules:
  0.0 288.2 jit_solution(5801843263021535777)
XLA Ops:
  12.5 10.7 %all_to_all.19 = bf16[4,224,160]{1,2,0:T(8,128)(2,1)S(1)} all-to-all(bf16[4,224,160]{1,2,0:T(8,128)(2,1)S(1)} %copy.56), channel_id=1, replica_groups=mesh['sec'=8,'dev'=4] {'dev'}, dimensions={0} | all-to-all | bytes 573440 | tf_op jit(solution)/shard_map/all_to_all | solution.py:356
  25.6 1.6 collective-permute-start.2
  27.2 1.4 collective-permute-start
  33.0 1.6 collective-permute-start.3
  34.6 2.0 collective-permute-done.3
  36.8 2.6 collective-permute-start.4
  39.4 1.9 collective-permute-done.4
  42.4 2.6 collective-permute-start.5
  45.0 12.2 %collective-permute-done.5 = bf16[4,80,320]{2,0,1:T(4,128)(2,1)S(1)} collective-permute-done((bf16[4,80,320]{2,0,1:T(4,128)(2,1)S(1)}, bf16[4,80,320]{2,0,1:T(4,128)(2,1)S(1)}, u32[]{:S(2)}, u32[]{:S(2)}) %collective-permute-start.5) | collective-permute-done | bytes 204832 | tf_op jit(solution)/shard_map/ppermute | solution.py:33
  57.8 10.0 %collective-permute-done.6 = bf16[2,80,320]{2,0,1:T(2,128)(2,1)S(1)} collective-permute-done((bf16[2,80,320]{2,0,1:T(2,128)(2,1)S(1)}, bf16[2,80,320]{2,0,1:T(2,128)(2,1)S(1)}, u32[]{:S(2)}, u32[]{:S(2)}) %collective-permute-start.6) | collective-permute-done | bytes 102432 | tf_op jit(solution)/shard_map/ppermute | solution.py:33
  70.0 3.5 %collective-permute-done.7 = bf16[1,80,320]{2,0,1:T(2,128)(2,1)S(1)} collective-permute-done((bf16[1,80,320]{2,0,1:T(2,128)(2,1)S(1)}, bf16[1,80,320]{2,0,1:T(2,128)(2,1)S(1)}, u32[]{:S(2)}, u32[]{:S(2)}) %collective-permute-start.7) | collective-permute-done | bytes 51232 | tf_op jit(solution)/shard_map/ppermute | solution.py:33
  76.7 1.6 collective-permute-start.9
  79.5 4.6 %collective-permute-done.9 = bf16[2,80,320]{2,0,1:T(2,128)(2,1)S(1)} collective-permute-done((bf16[2,80,320]{2,0,1:T(2,128)(2,1)S(1)}, bf16[2,80,320]{2,0,1:T(2,128)(2,1)S(1)}, u32[]{:S(2)}, u32[]{:S(2)}) %collective-permute-start.9) | collective-permute-done | bytes 102432 | tf_op jit(solution)/shard_map/ppermute | solution.py:33
  87.9 22.9 %all-gather.2.cloned.1.call-done = bf16[7168,640]{1,0:T(8,128)(2,1)} async-done(((bf16[224,640]{1,0:T(8,128)(2,1)}), bf16[7168,640]{1,0:T(8,128)(2,1)}) %all-gather.2.cloned.1.call-update) | async-done | bytes 9175056 | tf_op jit(solution)/shard_map/all_gather | solution.py:357
  112.7 70.8 %shard_map.210 = (f32[16,1024]{1,0:T(8,128)S(1)}, f32[16,640]{1,0:T(8,128)S(1)}) custom-call(f32[2]{0:T(128)S(1)} %add_convert_fusion.flags, f32[3,4]{1,0:T(4,128)S(1)} %copy-done.2, bf16[8,896,640]{2,1,0:T(8,128)(2,1)} %bitcast.129, f32[16,1536]{1,0:T(8,128)S(1)} %squeeze.18.x_in, f32[3,16,1536]{2,1,0:T(8,128)S(1)} %slice.134.noise, ...), custom_call_target="tpu_custom_call" | custom-call | flops 33973862400 | bytes 9830400 | tf_op jit(solution)/shard_map/pallas_call | solution.py:276
  183.5 2.2 collective-permute-start.10
  190.3 71.0 %shard_map.211 = (f32[16,1024]{1,0:T(8,128)S(1)}, f32[16,640]{1,0:T(8,128)S(1)}) custom-call(f32[2]{0:T(128)S(1)} %add_convert_fusion.flags, f32[3,4]{1,0:T(4,128)S(1)} %copy-done.1, bf16[8,896,640]{2,1,0:T(8,128)(2,1)} %bitcast.130, f32[16,1536]{1,0:T(8,128)S(1)} %pad_maximum_fusion.5.x_in, f32[3,16,1536]{2,1,0:T(8,128)S(1)} %slice.150.noise, ...), custom_call_target="tpu_custom_call" | custom-call | flops 33973862400 | bytes 9830400 | tf_op jit(solution)/shard_map/pallas_call | solution.py:276
  261.5 3.2 %collective-permute-start.12 = (f32[4,4,4,80]{3,2,1,0:T(4,128)S(1)}, f32[4,4,4,80]{3,2,1,0:T(4,128)S(1)}, u32[]{:S(2)}, u32[]{:S(2)}) collective-permute-start(f32[4,4,4,80]{3,2,1,0:T(4,128)S(1)} %slice_select_fusion), channel_id=1, source_target_pairs={{0,16},{4,20},{8,24},{12,28},{16,0},{20,4},{24,8},{28,12},{1,17},{... | collective-permute-start | bytes 61448 | tf_op jit(solution)/shard_map/ppermute | solution.py:33
  264.7 1.9 collective-permute-done.12
  266.6 2.4 collective-permute-start.13
  269.0 1.7 collective-permute-done.13
  270.8 1.6 collective-permute-start.14
  272.4 2.1 collective-permute-done.14
  274.5 3.5 %collective-permute-start.15 = (f32[2,4,80]{2,1,0:T(4,128)S(1)}, f32[2,4,80]{2,1,0:T(4,128)S(1)}, u32[]{:S(2)}, u32[]{:S(2)}) collective-permute-start(f32[2,4,80]{2,1,0:T(4,128)S(1)} %select_bitcast_fusion), channel_id=1, source_target_pairs={{0,2},{1,3},{2,0},{3,1},{4,6},{5,7},{6,4},{7,5},{8,10},{9,11},{10,... | collective-permute-start | bytes 7688 | tf_op jit(solution)/shard_map/ppermute | solution.py:33
  (164 shorter events, 31.1 us)
Async XLA Ops:
  7.2 103.6 %all-gather.2.cloned.1.call-start = ((), (), s32[]{:S(2)}) async-start(), calls=%async_computation.1 | async-start | bytes 9461760 | tf_op jit(solution)/shard_map/all_gather | solution.py:357
  25.6 7.3 %collective-permute-start.2 = (f32[1,2]{0,1:T(2,128)S(1)}, f32[1,2]{0,1:T(2,128)S(1)}, u32[]{:S(2)}, u32[]{:S(2)}) collective-permute-start(f32[1,2]{0,1:T(2,128)S(1)} %pad_maximum_fusion.7), channel_id=1, source_target_pairs={{0,4},{4,0},{8,12},{12,8},{16,20},{20,16},{24,28},{28,24},{1,5},{5... | collective-permute-start | bytes 32 | tf_op jit(solution)/shard_map/ppermute | solution.py:33
  27.2 46.5 %collective-permute-start = (f32[7,4,8,128]{3,2,1,0:T(8,128)S(1)}, f32[7,4,8,128]{3,2,1,0:T(8,128)S(1)}, u32[]{:S(2)}, u32[]{:S(2)}) collective-permute-start(f32[7,4,8,128]{3,2,1,0:T(8,128)S(1)} %get-tuple-element.24), channel_id=1, source_target_pairs={{0,1},{1,2},{2,3},{4,5},{5,6},{6,7},{8,9},{9,10},{10,11},{12,13},{... | collective-permute-start | bytes 344072 | tf_op jit(solution)/shard_map/ppermute | solution.py:70
  28.6 45.2 %collective-permute-start.1 = (f32[7,4,8,128]{3,2,1,0:T(8,128)S(1)}, f32[7,4,8,128]{3,2,1,0:T(8,128)S(1)}, u32[]{:S(2)}, u32[]{:S(2)}) collective-permute-start(f32[7,4,8,128]{3,2,1,0:T(8,128)S(1)} %get-tuple-element.25), channel_id=1, source_target_pairs={{1,0},{2,1},{3,2},{5,4},{6,5},{7,6},{9,8},{10,9},{11,10},{13,12},{... | collective-permute-start | bytes 344072 | tf_op jit(solution)/shard_map/ppermute | solution.py:71
  32.6 41.1 %copy-start.14 = (s32[128]{0:T(128)}, s32[128]{0:T(128)S(1)}, u32[]{:S(2)}) copy-start(s32[128]{0:T(128)S(1)} %fusion.30) | copy-start | bytes 1540
  33.0 3.6 %collective-permute-start.3 = (f32[2,2]{0,1:T(2,128)S(1)}, f32[2,2]{0,1:T(2,128)S(1)}, u32[]{:S(2)}, u32[]{:S(2)}) collective-permute-start(f32[2,2]{0,1:T(2,128)S(1)} %pad_maximum_fusion.8), channel_id=1, source_target_pairs={{0,8},{4,12},{8,0},{12,4},{16,24},{20,28},{24,16},{28,20},{1,9},{5... | collective-permute-start | bytes 56 | tf_op jit(solution)/shard_map/ppermute | solution.py:33
  36.8 4.5 %collective-permute-start.4 = (f32[4,2]{0,1:T(2,128)S(1)}, f32[4,2]{0,1:T(2,128)S(1)}, u32[]{:S(2)}, u32[]{:S(2)}) collective-permute-start(f32[4,2]{0,1:T(2,128)S(1)} %pad_maximum_fusion.9), channel_id=1, source_target_pairs={{0,16},{4,20},{8,24},{12,28},{16,0},{20,4},{24,8},{28,12},{1,17},{... | collective-permute-start | bytes 104 | tf_op jit(solution)/shard_map/ppermute | solution.py:33
  42.4 14.9 %collective-permute-start.5 = (bf16[4,80,320]{2,0,1:T(4,128)(2,1)S(1)}, bf16[4,80,320]{2,0,1:T(4,128)(2,1)S(1)}, u32[]{:S(2)}, u32[]{:S(2)}) collective-permute-start(bf16[4,80,320]{2,0,1:T(4,128)(2,1)S(1)} %select_convert_fusion), channel_id=1, source_target_pairs={{0,16},{4,20},{8,24},{12,28},{16,0},{20,4},{24,8},{28,12},{1,17},{... | collective-permute-start | bytes 614408 | tf_op jit(solution)/shard_map/ppermute | solution.py:33
  57.6 10.2 %collective-permute-start.6 = (bf16[2,80,320]{2,0,1:T(2,128)(2,1)S(1)}, bf16[2,80,320]{2,0,1:T(2,128)(2,1)S(1)}, u32[]{:S(2)}, u32[]{:S(2)}) collective-permute-start(bf16[2,80,320]{2,0,1:T(2,128)(2,1)S(1)} %select_convert_fusion.1), channel_id=1, source_target_pairs={{0,8},{4,12},{8,0},{12,4},{16,24},{20,28},{24,16},{28,20},{1,9},{5... | collective-permute-start | bytes 307208 | tf_op jit(solution)/shard_map/ppermute | solution.py:33
  68.2 5.3 %collective-permute-start.7 = (bf16[1,80,320]{2,0,1:T(2,128)(2,1)S(1)}, bf16[1,80,320]{2,0,1:T(2,128)(2,1)S(1)}, u32[]{:S(2)}, u32[]{:S(2)}) collective-permute-start(bf16[1,80,320]{2,0,1:T(2,128)(2,1)S(1)} %fusion.19), channel_id=1, source_target_pairs={{0,4},{4,0},{8,12},{12,8},{16,20},{20,16},{24,28},{28,24},{1,5},{5... | collective-permute-start | bytes 153608 | tf_op jit(solution)/shard_map/ppermute | solution.py:33
  73.7 1.5 collective-permute-start.8
  76.7 7.4 %collective-permute-start.9 = (bf16[2,80,320]{2,0,1:T(2,128)(2,1)S(1)}, bf16[2,80,320]{2,0,1:T(2,128)(2,1)S(1)}, u32[]{:S(2)}, u32[]{:S(2)}) collective-permute-start(bf16[2,80,320]{2,0,1:T(2,128)(2,1)S(1)} %pad_maximum_fusion.2), channel_id=1, source_target_pairs={{0,2},{1,3},{2,0},{3,1},{4,6},{5,7},{6,4},{7,5},{8,10},{9,11},{10,... | collective-permute-start | bytes 307208 | tf_op jit(solution)/shard_map/ppermute | solution.py:33
  87.1 25.5 %copy-start.2 = (f32[3,4]{1,0:T(4,128)S(1)}, f32[3,4]{1,0:T(4,128)}, u32[]{:S(2)}) copy-start(f32[3,4]{1,0:T(4,128)} %constant.103.factors) | copy-start | bytes 148
  112.6 74.4 %copy-start.18 = (f32[4]{0:T(128)S(1)}, f32[4]{0:T(128)}, u32[]{:S(2)}) copy-start(f32[4]{0:T(128)} %get-tuple-element.14) | copy-start | bytes 52
  112.6 74.4 %copy-start.19 = (f32[4]{0:T(128)S(1)}, f32[4]{0:T(128)}, u32[]{:S(2)}) copy-start(f32[4]{0:T(128)} %get-tuple-element.15) | copy-start | bytes 52
  112.6 74.4 %copy-start.20 = (f32[4]{0:T(128)S(1)}, f32[4]{0:T(128)}, u32[]{:S(2)}) copy-start(f32[4]{0:T(128)} %get-tuple-element.16) | copy-start | bytes 52
  112.6 77.6 %copy-start.1 = (f32[3,4]{1,0:T(4,128)S(1)}, f32[3,4]{1,0:T(4,128)}, u32[]{:S(2)}) copy-start(f32[3,4]{1,0:T(4,128)} %constant.102.factors) | copy-start | bytes 148
  183.5 6.7 %collective-permute-start.10 = (f32[16,256]{1,0:T(8,128)S(1)}, f32[16,256]{1,0:T(8,128)S(1)}, u32[]{:S(2)}, u32[]{:S(2)}) collective-permute-start(f32[16,256]{1,0:T(8,128)S(1)} %get-tuple-element.32), channel_id=1, source_target_pairs={{0,1},{1,2},{2,3},{4,5},{5,6},{6,7},{8,9},{9,10},{10,11},{12,13},{... | collective-permute-start | bytes 49160 | tf_op jit(solution)/shard_map/ppermute | solution.py:70
  185.7 4.6 %collective-permute-start.11 = (f32[16,256]{1,0:T(8,128)S(1)}, f32[16,256]{1,0:T(8,128)S(1)}, u32[]{:S(2)}, u32[]{:S(2)}) collective-permute-start(f32[16,256]{1,0:T(8,128)S(1)} %get-tuple-element.33), channel_id=1, source_target_pairs={{1,0},{2,1},{3,2},{5,4},{6,5},{7,6},{9,8},{10,9},{11,10},{13,12},{... | collective-permute-start | bytes 49160 | tf_op jit(solution)/shard_map/ppermute | solution.py:71
  261.5 5.0 %collective-permute-start.12 = (f32[4,4,4,80]{3,2,1,0:T(4,128)S(1)}, f32[4,4,4,80]{3,2,1,0:T(4,128)S(1)}, u32[]{:S(2)}, u32[]{:S(2)}) collective-permute-start(f32[4,4,4,80]{3,2,1,0:T(4,128)S(1)} %slice_select_fusion), channel_id=1, source_target_pairs={{0,16},{4,20},{8,24},{12,28},{16,0},{20,4},{24,8},{28,12},{1,17},{... | collective-permute-start | bytes 61448 | tf_op jit(solution)/shard_map/ppermute | solution.py:33
  266.6 4.2 %collective-permute-start.13 = (f32[2,4,4,80]{3,2,1,0:T(4,128)S(1)}, f32[2,4,4,80]{3,2,1,0:T(4,128)S(1)}, u32[]{:S(2)}, u32[]{:S(2)}) collective-permute-start(f32[2,4,4,80]{3,2,1,0:T(4,128)S(1)} %slice_select_fusion.1), channel_id=1, source_target_pairs={{0,8},{4,12},{8,0},{12,4},{16,24},{20,28},{24,16},{28,20},{1,9},{5... | collective-permute-start | bytes 30728 | tf_op jit(solution)/shard_map/ppermute | solution.py:33
  270.8 3.7 %collective-permute-start.14 = (f32[1,4,4,80]{3,2,1,0:T(4,128)S(1)}, f32[1,4,4,80]{3,2,1,0:T(4,128)S(1)}, u32[]{:S(2)}, u32[]{:S(2)}) collective-permute-start(f32[1,4,4,80]{3,2,1,0:T(4,128)S(1)} %slice_select_fusion.2), channel_id=1, source_target_pairs={{0,4},{4,0},{8,12},{12,8},{16,20},{20,16},{24,28},{28,24},{1,5},{5... | collective-permute-start | bytes 15368 | tf_op jit(solution)/shard_map/ppermute | solution.py:33
  274.5 5.0 %collective-permute-start.15 = (f32[2,4,80]{2,1,0:T(4,128)S(1)}, f32[2,4,80]{2,1,0:T(4,128)S(1)}, u32[]{:S(2)}, u32[]{:S(2)}) collective-permute-start(f32[2,4,80]{2,1,0:T(4,128)S(1)} %select_bitcast_fusion), channel_id=1, source_target_pairs={{0,2},{1,3},{2,0},{3,1},{4,6},{5,7},{6,4},{7,5},{8,10},{9,11},{10,... | collective-permute-start | bytes 7688 | tf_op jit(solution)/shard_map/ppermute | solution.py:33
  279.6 1.2 collective-permute-start.16
  (16 other events, 190.7 us)
Sparse Core Ops, SparseCore 0:
  24.3 86.3 all-gather.1
where the time goes:
time: 289 us; the launch traced here: 288 us
  Pallas kernels  142 us (49%)
  waiting for transfers between devices  64.4 us (22%)
  starting transfers between devices  28.1 us (10%)
  between operations  17.6 us (6%)
  local copies, waits for them, and re-layouts  15.7 us (5%)
  blocking collectives  10.7 us (4%)
  other arithmetic  7.5 us (3%)
    pallas_call x2, Pallas kernels, run_steps(): pl.pallas_call(functools.partial(steps_kernel, rows, cols, counts), out_s...  142 us
    ppermute x13, waiting for transfers between devices, swap(): return lax.ppermute(value, axis, [(i, i ^ mask) for i in range(size)])  41.6 us
    all_gather x1, waiting for transfers between devices, per_device(): packed = lax.all_gather(block, ('sec', 'dev'), axis=0, tiled=True)  22.9 us
    ppermute x13, starting transfers between devices, swap(): return lax.ppermute(value, axis, [(i, i ^ mask) for i in range(size)])  21.9 us
    all_to_all x1, blocking collectives, per_device(): lax.all_to_all(block, 'dev', split_axis=0, concat_axis=1, tiled=True)  10.7 us
  transfers between devices with their start and end apart: 18, of which 12 were waited for; matrix products, arithmetic and copies ran while one was open for 6% of the time, Pallas kernels for 0%

commit v1 on v0

--- a/solution.py
+++ b/solution.py
@@ -106,93 +106,156 @@
     return 0.5 * values * (1.0 + jnp.tanh(0.5 * values))
 
 
+def weight_copies(core, counts, sources, targets, sems):
+    if len(sources) == 1:
+        blocks = [(sources[0].at[part], 0, part) for part in range(sources[0].shape[0])]
+        length = sources[0].shape[1]
+    else:
+        parts, halves, length, _ = sources[0].shape
+        blocks = [
+            (sources[0 if c == core else 1].at[part, half], (2 * half + c) * length, part)
+            for part in range(parts)
+            for half in range(halves)
+            for c in range(2)
+        ]
+    copies = ([], [], [])
+    for block, first, part in blocks:
+        offset = 0
+        for which, (count, target) in enumerate(zip(counts, targets)):
+            low, high = max(first, offset), min(first + length, offset + count)
+            if low < high:
+                copies[which].append(
+                    pltpu.make_async_copy(
+                        block.at[pl.ds(low - first, high - low)],
+                        target.at[pl.ds(part * count + low - offset, high - low)],
+                        sems.at[which, len(copies[which])],
+                    )
+                )
+            offset += count
+    return copies
+
+
 def steps_kernel(
     rows,
     cols,
     counts,
+    source_count,
     flags,
     factors,
-    packed,
-    x_in,
-    noise,
-    key_blocks,
-    value_blocks,
-    bias,
-    gains,
-    w_in,
-    w_final,
-    x_out,
-    grad_out,
-    w_conv,
-    w_query,
-    w_attn,
-    hidden,
-    columns,
-    state,
-    sems,
+    *refs,
 ):
+    sources = refs[:source_count]
+    (
+        x_in,
+        noise,
+        key_blocks,
+        value_blocks,
+        bias,
+        gains,
+        w_in,
+        w_final,
+        x_out,
+        grad_out,
+        w_conv,
+        w_plus,
+        w_query,
+        w_attn,
+        hidden,
+        columns,
+        state,
+        sems,
+    ) = refs[source_count:]
     group = bias.shape[0]
     feats, chans = w_in.shape
-    parts = packed.shape[0]
-    copies = []
-    offset = 0
-    for which, (count, ref) in enumerate(zip(counts, (w_conv, w_query, w_attn))):
-        copies.append([])
-        for part in range(parts):
-            copy = pltpu.make_async_copy(
-                packed.at[part, pl.ds(offset, count)],
-                ref.at[pl.ds(part * count, count)],
-                sems.at[which, part],
-            )
-            copy.start()
-            copies[-1].append(copy)
-        offset += count
+    targets = (w_conv, w_query, w_attn)
+
+    def each_core(act):
+        if source_count == 1:
+            act(weight_copies(0, counts, sources, targets, sems))
+            return
+        for core in range(2):
+
+            @pl.when(flags[2] == core)
+            def _():
+                act(weight_copies(core, counts, sources, targets, sems))
+
+    def start_all(copies):
+        for some in copies:
+            for copy in some:
+                copy.start()
+
+    def wait_all(copies):
+        for some in copies:
+            for copy in some:
+                copy.wait()
+
+    each_core(start_all)
     state[...] = x_in[...]
     grad_out[...] = jnp.zeros_like(grad_out)
+    columns[...] = jnp.zeros_like(columns)
     pairs = key_blocks.shape[0]
     wide = 2 * HEAD
     size = CHUNK_ROWS * cols
     token = lax.broadcasted_iota(jnp.int32, (size, 1), 0)
     lane_token = lax.broadcasted_iota(jnp.int32, (1, size), 1)
     col = lax.rem(token, cols)
+    taps = 3 * chans
 
     def activate(step, chunk):
         start = pl.multiple_of(chunk * size, size)
-        span = pl.ds(start, size)
         before_norm = (
             lax.dot_general(
-                state[:, span].astype(jnp.bfloat16),
+                state[:, pl.ds(start, size)].astype(jnp.bfloat16),
                 w_in[...],
                 (((0,), (0,)), ((), ())),
                 preferred_element_type=jnp.float32,
             )
             + bias[pl.ds(step, 1), :]
         )
-        hidden[span, :] = before_norm
+        first = chunk * (CHUNK_ROWS // 2)
+        hidden[pl.ds(first, CHUNK_ROWS // 2)] = before_norm.reshape(
+            CHUNK_ROWS // 2, 2, cols, chans
+        )
         act = silu(rms_scale(before_norm, gains[0:1, :]))
         inside = jnp.where(
             start + token < HALO * cols,
             flags[0],
-            jnp.where(start + token >= (HALO + rows) * cols, flags[1], 1.0),
-        )
-        act = act * inside
+            jnp.where(start + token >= (HALO + rows) * cols, flags[1], 1),
+        )
+        act = act * inside.astype(jnp.float32)
         left = jnp.where(col == 0, 0.0, pltpu.roll(act, 1, 0))
         right = jnp.where(col == cols - 1, 0.0, pltpu.roll(act, size - 1, 0))
-        columns[span, 0:chans] = left.astype(jnp.bfloat16)
-        columns[span, chans : 2 * chans] = act.astype(jnp.bfloat16)
-        columns[span, 2 * chans : 3 * chans] = right.astype(jnp.bfloat16)
-
-    def convolve(start):
-        mixed = hidden[pl.ds(start, size), :]
-        for dr in range(3):
-            mixed = mixed + jnp.dot(
-                columns[pl.ds(start + (dr - 1) * cols, size), :],
-                w_conv[dr * 3 * chans : (dr + 1) * 3 * chans, :],
-                preferred_element_type=jnp.float32,
+        for which, value in enumerate((left, act, right)):
+            value = value.astype(jnp.bfloat16)
+            for row in range(CHUNK_ROWS):
+                columns[
+                    first + (row + 1) // 2, (row + 1) % 2, :, which * chans : (which + 1) * chans
+                ] = value[row * cols : (row + 1) * cols]
+
+    twos = (rows + HALO) // 4
+
+    def convolve(part, carry):
+        at = 1 + part * twos
+        above, upper = columns[pl.ds(at, twos), 0], columns[pl.ds(at, twos), 1]
+        lower, below = columns[pl.ds(at + 1, twos), 0], columns[pl.ds(at + 1, twos), 1]
+
+        def product(value, weight):
+            return jnp.dot(
+                value.reshape(twos * cols, taps), weight, preferred_element_type=jnp.float32
             )
-        return mixed
-
-    def finish(step, start, mixed):
+
+        plus = product(upper + lower, w_plus[...])
+        minus = product(lower - upper, w_conv[taps : 2 * taps, :])
+        span = pl.ds(at, twos)
+        even = plus + minus + product(above - lower, w_conv[:taps, :])
+        hidden[span, 0] += even.reshape(twos, cols, chans)
+        odd = plus - minus - product(upper - below, w_conv[2 * taps :, :])
+        hidden[span, 1] += odd.reshape(twos, cols, chans)
+        return carry
+
+    def finish(step, start):
+        row_pair = lax.div(start, 2 * cols)
+        mixed = hidden[pl.ds(row_pair, CHUNK_ROWS // 2)].reshape(size, chans)
         normed = rms_scale(mixed, gains[1:2, :]).astype(jnp.bfloat16)
         queries = jnp.dot(normed, w_query[...], preferred_element_type=jnp.float32).astype(
             jnp.bfloat16
@@ -239,64 +302,77 @@
             return carry
 
         lax.fori_loop(0, chunks, fill, 0)
+
+        @pl.when(step == 0)
+        def _():
+            each_core(wait_all)
+            block = chans // 5
+
+            def combine(number, carry):
+                here = pl.multiple_of(number * block, block)
+                first, middle, final = (
+                    w_conv[pl.ds(tap * taps + here, block), :].astype(jnp.float32)
+                    for tap in range(3)
+                )
+                outer = 0.5 * (first + final)
+                w_plus[pl.ds(here, block), :] = (outer + 0.5 * middle).astype(jnp.bfloat16)
+                w_conv[pl.ds(taps + here, block), :] = (outer - 0.5 * middle).astype(
+                    jnp.bfloat16
+                )
+                return carry
+
+            lax.fori_loop(0, taps // block, combine, 0)
+
+        lax.fori_loop(0, 2, convolve, 0)
         last = step == group - 1
         base = jnp.where(last, HALO, HALO // 2) * cols
-        count = jnp.where(last, chunks - 2, chunks - 1)
-
-        @pl.when(step == 0)
-        def _():
-            for some in copies:
-                for copy in some:
-                    copy.wait()
-
-        def place(number):
-            return pl.multiple_of(base + number * size, 2 * cols)
-
-        def body(number, mixed):
-            following = convolve(place(number))
-            finish(step, place(number - 1), mixed)
-            return following
-
-        mixed = lax.fori_loop(1, count, body, convolve(place(0)))
-        finish(step, place(count - 1), mixed)
+
+        def rest(number, carry):
+            finish(step, pl.multiple_of(base + number * size, 2 * cols))
+            return carry
+
+        lax.fori_loop(0, jnp.where(last, chunks - 2, chunks - 1), rest, 0)
         return carry
 
     lax.fori_loop(0, group, one_step, 0)
     x_out[...] = state[:, HALO * cols : (HALO + rows) * cols]
 
 
-def run_steps(rows, cols, counts, flags, factors, packed, x, noise, rest, bias):
+def run_steps(rows, cols, counts, flags, factors, sources, x, noise, rest, bias):
     key_blocks, value_blocks, gains, w_in, w_final = rest
     feats, chans = w_in.shape
-    parts = packed.shape[0]
-    tall = (rows + 2 * HALO) * cols
+    tall_rows = rows + 2 * HALO
     vmem = pl.BlockSpec(memory_space=pltpu.VMEM)
     smem = pl.BlockSpec(memory_space=pltpu.SMEM)
     token_rows = sum(rows + 2 * k for k in range(GROUP)) * cols
+    most = sources[0].shape[0] * (1 if len(sources) == 1 else 2 * sources[0].shape[1])
     return pl.pallas_call(
-        functools.partial(steps_kernel, rows, cols, counts),
+        functools.partial(steps_kernel, rows, cols, counts, len(sources)),
         out_shape=(
             jax.ShapeDtypeStruct((feats, rows * cols), jnp.float32),
             jax.ShapeDtypeStruct((feats, chans), jnp.float32),
         ),
-        in_specs=[smem, smem, pl.BlockSpec(memory_space=pl.ANY)] + [vmem] * 8,
+        in_specs=[smem, smem]
+        + [pl.BlockSpec(memory_space=pl.ANY)] * len(sources)
+        + [vmem] * 8,
         out_specs=(vmem, vmem),
         scratch_shapes=[
             pltpu.VMEM((9 * chans, chans), jnp.bfloat16),
+            pltpu.VMEM((3 * chans, chans), jnp.bfloat16),
             pltpu.VMEM((chans, chans), jnp.bfloat16),
             pltpu.VMEM((chans, chans), jnp.bfloat16),
-            pltpu.VMEM((tall, chans), jnp.float32),
-            pltpu.VMEM((tall, 3 * chans), jnp.bfloat16),
-            pltpu.VMEM((feats, tall), jnp.float32),
-            pltpu.SemaphoreType.DMA((3, parts)),
+            pltpu.VMEM((tall_rows // 2, 2, cols, chans), jnp.float32),
+            pltpu.VMEM((tall_rows // 2 + 1, 2, cols, 3 * chans), jnp.bfloat16),
+            pltpu.VMEM((feats, tall_rows * cols), jnp.float32),
+            pltpu.SemaphoreType.DMA((3, most)),
         ],
-        compiler_params=pltpu.CompilerParams(vmem_limit_bytes=48 * 2**20),
+        compiler_params=pltpu.CompilerParams(vmem_limit_bytes=52 * 2**20),
         cost_estimate=pl.CostEstimate(
             flops=2 * token_rows * chans * chans * 12,
             bytes_accessed=12 * chans * chans * 2,
             transcendentals=4 * token_rows * chans,
         ),
-    )(flags, factors, packed, x, noise, key_blocks, value_blocks, bias, gains, w_in, w_final)
+    )(flags, factors, *sources, x, noise, key_blocks, value_blocks, bias, gains, w_in, w_final)
 
 
 def advantages(onehot, own, rewards, own_reward):
@@ -354,13 +430,30 @@
     pieces.append(jnp.zeros((padded - used, col_piece), jnp.bfloat16))
     block = jnp.concatenate(pieces, axis=0)
     block = lax.all_to_all(block, "dev", split_axis=0, concat_axis=1, tiled=True)
-    packed = lax.all_gather(block, ("sec", "dev"), axis=0, tiled=True)
-    packed = packed.reshape(sec_count, padded, chans)
+    total = sec_count * dev_count
+    mates = [list(range(core, total, 2)) for core in range(2)]
+    mine = lax.all_gather(block, ("sec", "dev"), axis=0, tiled=True, axis_index_groups=mates)
+    theirs = swap(mine, "dev", 1)
+    core = lax.axis_index("dev") % 2
+    length = padded // dev_count
+    mine = mine.reshape(sec_count, dev_count // 2, length, chans)
+    theirs = theirs.reshape(mine.shape)
+
+    def rows_of(first, count, local):
+        if local and first // length == (first + count - 1) // length:
+            half, which = divmod(first // length, 2)
+            inner = slice(first % length, first % length + count)
+            return jnp.where(core == which, mine[:, half, inner], theirs[:, half, inner])
+        everything = jnp.where(
+            core == 0, jnp.stack([mine, theirs], axis=2), jnp.stack([theirs, mine], axis=2)
+        )
+        return everything.reshape(sec_count, padded, chans)[:, first : first + count]
+
     at = counts[0] + counts[1] + counts[2]
-    in_full = packed[:, at : at + counts[3]].reshape(feats, chans)
-    at += counts[3]
+    small = rows_of(at, counts[3] + counts[4], True)
+    in_full = small[:, : counts[3]].reshape(feats, chans)
     final_full = (
-        packed[:, at : at + counts[4]]
+        small[:, counts[3] :]
         .reshape(sec_count, counts[4], dev_count, col_piece)
         .transpose(0, 2, 1, 3)
         .reshape(sec_count, dev_count, chans // sec_count, feats // dev_count)
@@ -368,14 +461,14 @@
         .reshape(chans, feats)
     )
     big = counts[:3]
+    sources = (mine, theirs)
     if any(count % 16 for count in big):
-        packed = jnp.concatenate(
-            [
-                packed[:, sum(big[:k]) : sum(big[: k + 1])].reshape(-1, chans)
-                for k in range(3)
-            ],
-            axis=0,
-        )[None]
+        first = [sum(big[:k]) for k in range(3)]
+        sources = (
+            jnp.concatenate(
+                [rows_of(f, c, False).reshape(-1, chans) for f, c in zip(first, big)], axis=0
+            )[None],
+        )
         big = [count * sec_count for count in big]
 
     both = jnp.stack([rewards, prompt_ids.astype(jnp.float32)], axis=1)
@@ -427,7 +520,7 @@
     )
 
     position = lax.axis_index("dev")
-    flags = jnp.stack([position > 0, position < dev_count - 1]).astype(jnp.float32)
+    flags = jnp.stack([position > 0, position < dev_count - 1, core == 1]).astype(jnp.int32)
     planes = jnp.concatenate([latents, noise[:, 0]], axis=0)
     planes = to_tokens(with_halo(planes, "dev", 2, 2 * HALO))
     x, noise_wide = planes[0], planes[1:]
@@ -447,7 +540,7 @@
             big,
             flags,
             factors[part],
-            packed,
+            sources,
             x,
             noise_wide[part],
             rest,
@@ -459,8 +552,9 @@
     gradient = gradient * advantage
     row_piece = chans // sec_count
     arranged = gradient.reshape(dev_count, feats // dev_count, sec_count, row_piece)
-    arranged = arranged.transpose(2, 0, 1, 3)
-    grad_shard = halved_sum(halved_sum(arranged, "sec")[0], "dev")[0].T
+    arranged = arranged.transpose(2, 0, 1, 3).reshape(total, -1)
+    arrived = lax.all_to_all(arranged, ("sec", "dev"), split_axis=0, concat_axis=0, tiled=True)
+    grad_shard = jnp.sum(arrived, axis=0).reshape(feats // dev_count, row_piece).T
     grad_shard = -grad_shard / sec_count
     moment_one = 0.9 * moment_first + 0.1 * grad_shard
     moment_two = 0.999 * moment_second + 0.001 * grad_shard * grad_shard

time: 289 us -> 304 us (1.052)
  waiting for transfers between devices: 64.4 us -> 95.3 us
  Pallas kernels: 142 us -> 130 us
  starting transfers between devices: 28.1 us -> 22.5 us
    all_gather x1, waiting for transfers between devices: 22.9 us -> 62 us  [per_device(): lax.all_gather(block, ('sec', 'dev'), axis=0, tiled=True, axis_index_grou...]
    ppermute x13 -> x9, waiting for transfers between devices: 41.6 us -> 27.1 us  [swap(): return lax.ppermute(value, axis, [(i, i ^ mask) for i in range(size)])]
    pallas_call x2, Pallas kernels: 142 us -> 130 us  [run_steps(): pl.pallas_call(functools.partial(steps_kernel, rows, cols, counts, len(so...]
    ppermute x13 -> x9, starting transfers between devices: 21.9 us -> 11 us  [swap(): return lax.ppermute(value, axis, [(i, i ^ mask) for i in range(size)])]
    all_to_all x0 -> x1, waiting for transfers between devices: none -> 6.19 us  [per_device(): lax.all_to_all(arranged, ('sec', 'dev'), split_axis=0, concat_axis=0, til...]
    all_to_all x0 -> x1, starting transfers between devices: none -> 5.91 us  [per_device(): lax.all_to_all(arranged, ('sec', 'dev'), split_axis=0, concat_axis=0, til...]
  transfers between devices with their start and end apart: 18 -> 15, of which waited for: 12 -> 8; matrix products, arithmetic and copies ran while one was open for 6% -> 6% of each run, Pallas kernels for 0% -> 0%
where the time goes in v1:
time: 304 us
  Pallas kernels  130 us (43%)
  waiting for transfers between devices  95.3 us (31%)
  starting transfers between devices  22.5 us (7%)
  between operations  17.5 us (6%)
  local copies, waits for them, and re-layouts  15.5 us (5%)
  blocking collectives  10.7 us (4%)
  other arithmetic  8.83 us (3%)
  matrix products  3.22 us (1%)
    pallas_call x2, Pallas kernels, run_steps(): pl.pallas_call(functools.partial(steps_kernel, rows, cols, counts, len(so...  130 us
    all_gather x1, waiting for transfers between devices, per_device(): lax.all_gather(block, ('sec', 'dev'), axis=0, tiled=True, axis_index_grou...  62 us
    ppermute x9, waiting for transfers between devices, swap(): return lax.ppermute(value, axis, [(i, i ^ mask) for i in range(size)])  27.1 us
    ppermute x9, starting transfers between devices, swap(): return lax.ppermute(value, axis, [(i, i ^ mask) for i in range(size)])  11 us
    all_to_all x1, blocking collectives, per_device(): lax.all_to_all(block, 'dev', split_axis=0, concat_axis=1, tiled=True)  10.7 us
    all_to_all x1, waiting for transfers between devices, per_device(): lax.all_to_all(arranged, ('sec', 'dev'), split_axis=0, concat_axis=0, til...  6.19 us
  transfers between devices with their start and end apart: 15, of which 8 were waited for; matrix products, arithmetic and copies ran while one was open for 6% of the time, Pallas kernels for 0%

profile of v1, /device:TPU:0, one launch (start us, length us, event | category | flops | bytes accessed | tf_op | source)
XLA Modules:
  0.0 303.7 jit_solution(11876416207629684678)
XLA Ops:
  12.5 10.7 %all_to_all.29 = bf16[4,224,160]{1,2,0:T(8,128)(2,1)S(1)} all-to-all(bf16[4,224,160]{1,2,0:T(8,128)(2,1)S(1)} %copy.56), channel_id=1, replica_groups=mesh['sec'=8,'dev'=4] {'dev'}, dimensions={0} | all-to-all | bytes 573440 | tf_op jit(solution)/shard_map/all_to_all | solution.py:432
  25.5 1.6 collective-permute-start.3
  27.1 1.4 collective-permute-start.1
  28.5 1.3 collective-permute-start.2
  33.4 1.6 collective-permute-start.4
  35.0 2.0 collective-permute-done.4
  37.2 2.6 collective-permute-start.5
  39.8 1.9 collective-permute-done.5
  41.8 62.0 %all-gather.2.cloned.1.call-done = bf16[3584,640]{1,0:T(8,128)(2,1)} async-done(((bf16[224,640]{1,0:T(8,128)(2,1)}), bf16[3584,640]{1,0:T(8,128)(2,1)}) %all-gather.2.cloned.1.call-update) | async-done | bytes 4587536 | tf_op jit(solution)/shard_map/all_gather | solution.py:435
  104.8 2.0 collective-permute-start.6
  106.8 12.5 %collective-permute-done.6 = bf16[4,80,320]{2,0,1:T(4,128)(2,1)S(1)} collective-permute-done((bf16[4,80,320]{2,0,1:T(4,128)(2,1)S(1)}, bf16[4,80,320]{2,0,1:T(4,128)(2,1)S(1)}, u32[]{:S(2)}, u32[]{:S(2)}) %collective-permute-start.6) | collective-permute-done | bytes 204832 | tf_op jit(solution)/shard_map/ppermute | solution.py:33
  119.9 4.9 %collective-permute-done.7 = bf16[2,80,320]{2,0,1:T(2,128)(2,1)S(1)} collective-permute-done((bf16[2,80,320]{2,0,1:T(2,128)(2,1)S(1)}, bf16[2,80,320]{2,0,1:T(2,128)(2,1)S(1)}, u32[]{:S(2)}, u32[]{:S(2)}) %collective-permute-start.7) | collective-permute-done | bytes 102432 | tf_op jit(solution)/shard_map/ppermute | solution.py:33
  125.1 1.5 collective-permute-start.8
  127.3 2.7 collective-permute-done.8
  130.4 1.3 fusion
  134.2 1.5 collective-permute-start.10
  136.9 3.0 collective-permute-done.10
  145.5 65.1 %shard_map.210 = (f32[16,1024]{1,0:T(8,128)S(1)}, f32[16,640]{1,0:T(8,128)S(1)}) custom-call(s32[3]{0:T(128)S(1)} %add_convert_fusion.flags, f32[3,4]{1,0:T(4,128)S(1)} %copy-done.2, bf16[8,2,224,640]{3,2,1,0:T(8,128)(2,1)} %bitcast.124, bf16[8,2,224,640]{3,2,1,0:T(8,128)(2,1)} %bitcast.6.refs_1_, f32[16,1536]{1,0:T(8,128)S(1)} %squeeze.18.refs_2_, ...), custom_call_target="tpu_custom_call" | custom-call | flops 33973862400 | bytes 9830400 | tf_op jit(solution)/shard_map/pallas_call | solution.py:349
  210.5 1.6 collective-permute-start.11
  212.1 1.3 collective-permute-start.12
  215.4 1.2 slice.116.refs_3_
  216.7 65.1 %shard_map.211 = (f32[16,1024]{1,0:T(8,128)S(1)}, f32[16,640]{1,0:T(8,128)S(1)}) custom-call(s32[3]{0:T(128)S(1)} %add_convert_fusion.flags, f32[3,4]{1,0:T(4,128)S(1)} %copy-done.1, bf16[8,2,224,640]{3,2,1,0:T(8,128)(2,1)} %bitcast.125, bf16[8,2,224,640]{3,2,1,0:T(8,128)(2,1)} %bitcast.6.refs_1_, f32[16,1536]{1,0:T(8,128)S(1)} %pad_maximum_fusion.5.refs_2_, ...), custom_call_target="tpu_custom_call" | custom-call | flops 33973862400 | bytes 9830400 | tf_op jit(solution)/shard_map/pallas_call | solution.py:349
  282.8 5.9 %all-to-all-start.1 = ((f32[32,1,320]{2,1,0:T(1,128)}), f32[32,1,320]{2,1,0:T(1,128)S(1)}, u32[]{:S(2)}, u32[]{:S(2)}) async-start(f32[32,1,320]{2,1,0:T(1,128)} %all_to_all.26), calls=%async_computation.1 | async-start | bytes 98304 | tf_op jit(solution)/shard_map/all_to_all | solution.py:556
  289.8 6.2 %all-to-all-done.1 = f32[32,1,320]{2,1,0:T(1,128)S(1)} async-done(((f32[32,1,320]{2,1,0:T(1,128)}), f32[32,1,320]{2,1,0:T(1,128)S(1)}, u32[]{:S(2)}, u32[]{:S(2)}) %all-to-all-start.1) | async-done | bytes 40992 | tf_op jit(solution)/shard_map/all_to_all | solution.py:556
  (155 shorter events, 25.1 us)
Async XLA Ops:
  7.2 24.8 %copy-start = (bf16[4,77,2048]{2,0,1:T(4,128)(2,1)S(1)}, bf16[4,77,2048]{2,0,1:T(4,128)(2,1)}, u32[]{:S(2)}) copy-start(bf16[4,77,2048]{2,0,1:T(4,128)(2,1)} %param.23) | copy-start | bytes 3784708
  7.2 96.6 %all-gather.2.cloned.1.call-start = ((), (), s32[]{:S(2)}) async-start(), calls=%async_computation.2 | async-start | bytes 4874240 | tf_op jit(solution)/shard_map/all_gather | solution.py:435
  12.4 17.6 %copy-start.11 = (f32[640]{0:T(1024)S(1)}, f32[640]{0:T(1024)}, u32[]{:S(2)}) copy-start(f32[640]{0:T(1024)} %param.25) | copy-start | bytes 7684
  12.5 17.6 %copy-start.13 = (f32[640]{0:T(1024)S(1)}, f32[640]{0:T(1024)}, u32[]{:S(2)}) copy-start(f32[640]{0:T(1024)} %param.27) | copy-start | bytes 7684
  25.5 7.8 %collective-permute-start.3 = (f32[1,2]{0,1:T(2,128)S(1)}, f32[1,2]{0,1:T(2,128)S(1)}, u32[]{:S(2)}, u32[]{:S(2)}) collective-permute-start(f32[1,2]{0,1:T(2,128)S(1)} %pad_maximum_fusion.7), channel_id=1, source_target_pairs={{0,4},{4,0},{8,12},{12,8},{16,20},{20,16},{24,28},{28,24},{1,5},{5... | collective-permute-start | bytes 32 | tf_op jit(solution)/shard_map/ppermute | solution.py:33
  27.1 103.2 %collective-permute-start.1 = (f32[7,4,8,128]{3,2,1,0:T(8,128)S(1)}, f32[7,4,8,128]{3,2,1,0:T(8,128)S(1)}, u32[]{:S(2)}, u32[]{:S(2)}) collective-permute-start(f32[7,4,8,128]{3,2,1,0:T(8,128)S(1)} %get-tuple-element.22), channel_id=1, source_target_pairs={{0,1},{1,2},{2,3},{4,5},{5,6},{6,7},{8,9},{9,10},{10,11},{12,13},{... | collective-permute-start | bytes 344072 | tf_op jit(solution)/shard_map/ppermute | solution.py:70
  28.5 101.8 %collective-permute-start.2 = (f32[7,4,8,128]{3,2,1,0:T(8,128)S(1)}, f32[7,4,8,128]{3,2,1,0:T(8,128)}, u32[]{:S(2)}, u32[]{:S(2)}) collective-permute-start(f32[7,4,8,128]{3,2,1,0:T(8,128)S(1)} %get-tuple-element.23), channel_id=1, source_target_pairs={{1,0},{2,1},{3,2},{5,4},{6,5},{7,6},{9,8},{10,9},{11,10},{13,12},{... | collective-permute-start | bytes 344072 | tf_op jit(solution)/shard_map/ppermute | solution.py:71
  33.1 73.8 %copy-start.9 = (f32[6,640]{1,0:T(8,128)S(1)}, f32[6,640]{1,0:T(8,128)}, u32[]{:S(2)}) copy-start(f32[6,640]{1,0:T(8,128)} %param.24) | copy-start | bytes 46084
  33.4 3.6 %collective-permute-start.4 = (f32[2,2]{0,1:T(2,128)S(1)}, f32[2,2]{0,1:T(2,128)S(1)}, u32[]{:S(2)}, u32[]{:S(2)}) collective-permute-start(f32[2,2]{0,1:T(2,128)S(1)} %pad_maximum_fusion.8), channel_id=1, source_target_pairs={{0,8},{4,12},{8,0},{12,4},{16,24},{20,28},{24,16},{28,20},{1,9},{5... | collective-permute-start | bytes 56 | tf_op jit(solution)/shard_map/ppermute | solution.py:33
  37.2 4.5 %collective-permute-start.5 = (f32[4,2]{0,1:T(2,128)S(1)}, f32[4,2]{0,1:T(2,128)S(1)}, u32[]{:S(2)}, u32[]{:S(2)}) collective-permute-start(f32[4,2]{0,1:T(2,128)S(1)} %pad_maximum_fusion.9), channel_id=1, source_target_pairs={{0,16},{4,20},{8,24},{12,28},{16,0},{20,4},{24,8},{28,12},{1,17},{... | collective-permute-start | bytes 104 | tf_op jit(solution)/shard_map/ppermute | solution.py:33
  103.8 39.8 %collective-permute-start = (bf16[3584,640]{1,0:T(8,128)(2,1)}, bf16[3584,640]{1,0:T(8,128)(2,1)}, u32[]{:S(2)}, u32[]{:S(2)}) collective-permute-start(bf16[3584,640]{1,0:T(8,128)(2,1)} %all-gather.2.cloned.1.call-done), channel_id=1, source_target_pairs={{0,1},{1,0},{2,3},{3,2},{4,5},{5,4},{6,7},{7,6},{8,9},{9,8},{10,11... | collective-permute-start | bytes 13762568 | tf_op jit(solution)/shard_map/ppermute | solution.py:33
  104.8 14.6 %collective-permute-start.6 = (bf16[4,80,320]{2,0,1:T(4,128)(2,1)S(1)}, bf16[4,80,320]{2,0,1:T(4,128)(2,1)S(1)}, u32[]{:S(2)}, u32[]{:S(2)}) collective-permute-start(bf16[4,80,320]{2,0,1:T(4,128)(2,1)S(1)} %select_convert_fusion), channel_id=1, source_target_pairs={{0,16},{4,20},{8,24},{12,28},{16,0},{20,4},{24,8},{28,12},{1,17},{... | collective-permute-start | bytes 614408 | tf_op jit(solution)/shard_map/ppermute | solution.py:33
  119.8 5.0 %collective-permute-start.7 = (bf16[2,80,320]{2,0,1:T(2,128)(2,1)S(1)}, bf16[2,80,320]{2,0,1:T(2,128)(2,1)S(1)}, u32[]{:S(2)}, u32[]{:S(2)}) collective-permute-start(bf16[2,80,320]{2,0,1:T(2,128)(2,1)S(1)} %select_convert_fusion.1), channel_id=1, source_target_pairs={{0,8},{4,12},{8,0},{12,4},{16,24},{20,28},{24,16},{28,20},{1,9},{5... | collective-permute-start | bytes 307208 | tf_op jit(solution)/shard_map/ppermute | solution.py:33
  125.1 4.9 %collective-permute-start.8 = (bf16[1,80,320]{2,0,1:T(2,128)(2,1)S(1)}, bf16[1,80,320]{2,0,1:T(2,128)(2,1)S(1)}, u32[]{:S(2)}, u32[]{:S(2)}) collective-permute-start(bf16[1,80,320]{2,0,1:T(2,128)(2,1)S(1)} %fusion.19), channel_id=1, source_target_pairs={{0,4},{4,0},{8,12},{12,8},{16,20},{20,16},{24,28},{28,24},{1,5},{5... | collective-permute-start | bytes 153608 | tf_op jit(solution)/shard_map/ppermute | solution.py:33
  130.3 2.4 collective-permute-start.9
  134.2 5.8 %collective-permute-start.10 = (bf16[2,80,320]{2,0,1:T(2,128)(2,1)S(1)}, bf16[2,80,320]{2,0,1:T(2,128)(2,1)S(1)}, u32[]{:S(2)}, u32[]{:S(2)}) collective-permute-start(bf16[2,80,320]{2,0,1:T(2,128)(2,1)S(1)} %pad_maximum_fusion.2), channel_id=1, source_target_pairs={{0,2},{1,3},{2,0},{3,1},{4,6},{5,7},{6,4},{7,5},{8,10},{9,11},{10,... | collective-permute-start | bytes 307208 | tf_op jit(solution)/shard_map/ppermute | solution.py:33
  145.4 68.0 %copy-start.16 = (f32[4]{0:T(128)S(1)}, f32[4]{0:T(128)}, u32[]{:S(2)}) copy-start(f32[4]{0:T(128)} %get-tuple-element.14) | copy-start | bytes 52
  145.4 68.0 %copy-start.17 = (f32[4]{0:T(128)S(1)}, f32[4]{0:T(128)}, u32[]{:S(2)}) copy-start(f32[4]{0:T(128)} %get-tuple-element.15) | copy-start | bytes 52
  145.4 68.0 %copy-start.18 = (f32[4]{0:T(128)S(1)}, f32[4]{0:T(128)}, u32[]{:S(2)}) copy-start(f32[4]{0:T(128)} %get-tuple-element.16) | copy-start | bytes 52
  145.5 71.3 %copy-start.1 = (f32[3,4]{1,0:T(4,128)S(1)}, f32[3,4]{1,0:T(4,128)}, u32[]{:S(2)}) copy-start(f32[3,4]{1,0:T(4,128)} %constant.111.factors) | copy-start | bytes 148
  210.5 6.1 %collective-permute-start.11 = (f32[16,256]{1,0:T(8,128)S(1)}, f32[16,256]{1,0:T(8,128)S(1)}, u32[]{:S(2)}, u32[]{:S(2)}) collective-permute-start(f32[16,256]{1,0:T(8,128)S(1)} %get-tuple-element.30), channel_id=1, source_target_pairs={{0,1},{1,2},{2,3},{4,5},{5,6},{6,7},{8,9},{9,10},{10,11},{12,13},{... | collective-permute-start | bytes 49160 | tf_op jit(solution)/shard_map/ppermute | solution.py:70
  212.1 4.6 %collective-permute-start.12 = (f32[16,256]{1,0:T(8,128)S(1)}, f32[16,256]{1,0:T(8,128)S(1)}, u32[]{:S(2)}, u32[]{:S(2)}) collective-permute-start(f32[16,256]{1,0:T(8,128)S(1)} %get-tuple-element.31), channel_id=1, source_target_pairs={{1,0},{2,1},{3,2},{5,4},{6,5},{7,6},{9,8},{10,9},{11,10},{13,12},{... | collective-permute-start | bytes 49160 | tf_op jit(solution)/shard_map/ppermute | solution.py:71
  216.7 72.2 %copy-start.15 = (s32[128]{0:T(128)S(1)}, s32[128]{0:T(128)}, u32[]{:S(2)}) copy-start(s32[128]{0:T(128)} %fusion.31) | copy-start | bytes 1540
  282.8 13.2 %all-to-all-start.1 = ((f32[32,1,320]{2,1,0:T(1,128)}), f32[32,1,320]{2,1,0:T(1,128)S(1)}, u32[]{:S(2)}, u32[]{:S(2)}) async-start(f32[32,1,320]{2,1,0:T(1,128)} %all_to_all.26), calls=%async_computation.1 | async-start | bytes 98304 | tf_op jit(solution)/shard_map/all_to_all | solution.py:556
  (13 other events, 128.3 us)
Sparse Core Ops, SparseCore 0:
  24.3 79.4 all-gather.1

commit v2 on v1

--- a/solution.py
+++ b/solution.py
@@ -102,48 +102,58 @@
     return values * lax.rsqrt(mean_square + norm_eps) * gain
 
 
-def silu(values):
-    return 0.5 * values * (1.0 + jnp.tanh(0.5 * values))
-
-
-def weight_copies(core, counts, sources, targets, sems):
-    if len(sources) == 1:
-        blocks = [(sources[0].at[part], 0, part) for part in range(sources[0].shape[0])]
-        length = sources[0].shape[1]
-    else:
-        parts, halves, length, _ = sources[0].shape
-        blocks = [
-            (sources[0 if c == core else 1].at[part, half], (2 * half + c) * length, part)
-            for part in range(parts)
-            for half in range(halves)
-            for c in range(2)
-        ]
+def silu_of_twice(values):
+    return values + values * jnp.tanh(values)
+
+
+def weight_copies(counts, split, relative, flags, refs, targets, sems):
+    main, pieces = refs[0], refs[1:]
     copies = ([], [], [])
-    for block, first, part in blocks:
+
+    def add(which, source, target):
+        number = len(copies[which])
+        copies[which].append(pltpu.make_async_copy(source, target, sems.at[which, number]))
+
+    for part in range(main.shape[0]):
         offset = 0
         for which, (count, target) in enumerate(zip(counts, targets)):
-            low, high = max(first, offset), min(first + length, offset + count)
-            if low < high:
-                copies[which].append(
-                    pltpu.make_async_copy(
-                        block.at[pl.ds(low - first, high - low)],
-                        target.at[pl.ds(part * count + low - offset, high - low)],
-                        sems.at[which, len(copies[which])],
-                    )
-                )
-            offset += count
+            here = split if which == 0 else count
+            add(
+                which,
+                main.at[part, pl.ds(offset, here)],
+                target.at[pl.ds(part * count, here)],
+            )
+            offset += here
+    for piece, places in zip(pieces, relative):
+        for number, (sec, dev) in enumerate(places):
+            length = piece.shape[1]
+            row = (flags[2] ^ sec) * counts[0] + split + (flags[3] ^ dev) * length
+            row = pl.multiple_of(row, 16)
+            add(0, piece.at[number], targets[0].at[pl.ds(row, length)])
     return copies
+
+
+def interleave(*tasks):
+    tasks = list(tasks)
+    while tasks:
+        for task in list(tasks):
+            try:
+                next(task)
+            except StopIteration:
+                tasks.remove(task)
 
 
 def steps_kernel(
     rows,
     cols,
     counts,
-    source_count,
+    split,
+    relative,
     flags,
     factors,
     *refs,
 ):
+    source_count = 1 + len(relative)
     sources = refs[:source_count]
     (
         x_in,
@@ -167,42 +177,23 @@
     ) = refs[source_count:]
     group = bias.shape[0]
     feats, chans = w_in.shape
-    targets = (w_conv, w_query, w_attn)
-
-    def each_core(act):
-        if source_count == 1:
-            act(weight_copies(0, counts, sources, targets, sems))
-            return
-        for core in range(2):
-
-            @pl.when(flags[2] == core)
-            def _():
-                act(weight_copies(core, counts, sources, targets, sems))
-
-    def start_all(copies):
-        for some in copies:
-            for copy in some:
-                copy.start()
-
-    def wait_all(copies):
-        for some in copies:
-            for copy in some:
-                copy.wait()
-
-    each_core(start_all)
+    copies = weight_copies(
+        counts, split, relative, flags, sources, (w_conv, w_query, w_attn), sems
+    )
+    for some in copies:
+        for copy in some:
+            copy.start()
     state[...] = x_in[...]
     grad_out[...] = jnp.zeros_like(grad_out)
-    columns[...] = jnp.zeros_like(columns)
     pairs = key_blocks.shape[0]
     wide = 2 * HEAD
     size = CHUNK_ROWS * cols
-    token = lax.broadcasted_iota(jnp.int32, (size, 1), 0)
     lane_token = lax.broadcasted_iota(jnp.int32, (1, size), 1)
-    col = lax.rem(token, cols)
+    edge = 16
+    near = lax.broadcasted_iota(jnp.int32, (edge, 1), 0)
     taps = 3 * chans
 
-    def activate(step, chunk):
-        start = pl.multiple_of(chunk * size, size)
+    def activate(step, start):
         before_norm = (
             lax.dot_general(
                 state[:, pl.ds(start, size)].astype(jnp.bfloat16),
@@ -212,25 +203,32 @@
             )
             + bias[pl.ds(step, 1), :]
         )
-        first = chunk * (CHUNK_ROWS // 2)
-        hidden[pl.ds(first, CHUNK_ROWS // 2)] = before_norm.reshape(
-            CHUNK_ROWS // 2, 2, cols, chans
-        )
-        act = silu(rms_scale(before_norm, gains[0:1, :]))
-        inside = jnp.where(
-            start + token < HALO * cols,
-            flags[0],
-            jnp.where(start + token >= (HALO + rows) * cols, flags[1], 1),
-        )
-        act = act * inside.astype(jnp.float32)
-        left = jnp.where(col == 0, 0.0, pltpu.roll(act, 1, 0))
-        right = jnp.where(col == cols - 1, 0.0, pltpu.roll(act, size - 1, 0))
-        for which, value in enumerate((left, act, right)):
-            value = value.astype(jnp.bfloat16)
-            for row in range(CHUNK_ROWS):
-                columns[
-                    first + (row + 1) // 2, (row + 1) % 2, :, which * chans : (which + 1) * chans
-                ] = value[row * cols : (row + 1) * cols]
+        first = lax.div(start, 2 * cols)
+        yield
+        for row in range(CHUNK_ROWS):
+            value = before_norm[row * cols : (row + 1) * cols]
+            hidden[first + row // 2, row % 2] = value
+            act = silu_of_twice(rms_scale(value, gains[0:1, :]))
+            place = 2 * first + row
+            inside = jnp.where(
+                place < HALO, flags[0], jnp.where(place >= HALO + rows, flags[1], 1)
+            )
+            act = act * inside.astype(jnp.float32)
+            at = (first + (row + 1) // 2, (row + 1) % 2)
+            left = pltpu.roll(act, 1, 0)
+            right = pltpu.roll(act, cols - 1, 0)
+            first_left = jnp.where(near == 0, 0.0, left[:edge])
+            last_right = jnp.where(near == edge - 1, 0.0, right[cols - edge :])
+            columns[at + (slice(0, edge), slice(0, chans))] = first_left.astype(jnp.bfloat16)
+            columns[at + (slice(edge, cols), slice(0, chans))] = left[edge:].astype(jnp.bfloat16)
+            columns[at + (slice(0, cols), slice(chans, 2 * chans))] = act.astype(jnp.bfloat16)
+            columns[at + (slice(0, cols - edge), slice(2 * chans, taps))] = right[
+                : cols - edge
+            ].astype(jnp.bfloat16)
+            columns[at + (slice(cols - edge, cols), slice(2 * chans, taps))] = last_right.astype(
+                jnp.bfloat16
+            )
+            yield
 
     twos = (rows + HALO) // 4
 
@@ -257,9 +255,11 @@
         row_pair = lax.div(start, 2 * cols)
         mixed = hidden[pl.ds(row_pair, CHUNK_ROWS // 2)].reshape(size, chans)
         normed = rms_scale(mixed, gains[1:2, :]).astype(jnp.bfloat16)
+        yield
         queries = jnp.dot(normed, w_query[...], preferred_element_type=jnp.float32).astype(
             jnp.bfloat16
         )
+        yield
         heads = []
         for pair in range(pairs):
             scores = jnp.dot(
@@ -272,10 +272,15 @@
                 value_blocks[pair],
                 preferred_element_type=jnp.float32,
             )
-            heads.append((sums[:, :wide] / sums[:, wide:]).astype(jnp.bfloat16))
+            heads.append(
+                (sums[:, :wide] * pl.reciprocal(sums[:, wide:], approx=True)).astype(
+                    jnp.bfloat16
+                )
+            )
+            yield
         attended = jnp.concatenate(heads, axis=1)
         output = mixed + jnp.dot(attended, w_attn[...], preferred_element_type=jnp.float32)
-        act = silu(rms_scale(output, gains[2:3, :])).astype(jnp.bfloat16)
+        act = silu_of_twice(rms_scale(output, gains[2:3, :])).astype(jnp.bfloat16)
         predicted = jnp.dot(act, w_final[...], preferred_element_type=jnp.float32)
         span = pl.ds(start, size)
         noise_now = noise[step, :, span]
@@ -296,58 +301,66 @@
 
     chunks = state.shape[1] // size
 
+    def fill(chunk, carry):
+        interleave(activate(0, pl.multiple_of(chunk * size, size)))
+        return carry
+
+    lax.fori_loop(0, chunks, fill, 0)
+    for some in copies:
+        for copy in some:
+            copy.wait()
+    block = chans // 5
+
+    def combine(number, carry):
+        here = pl.multiple_of(number * block, block)
+        first, middle, final = (
+            w_conv[pl.ds(tap * taps + here, block), :].astype(jnp.float32) for tap in range(3)
+        )
+        outer = 0.5 * (first + final)
+        w_plus[pl.ds(here, block), :] = (outer + 0.5 * middle).astype(jnp.bfloat16)
+        w_conv[pl.ds(taps + here, block), :] = (outer - 0.5 * middle).astype(jnp.bfloat16)
+        return carry
+
+    lax.fori_loop(0, taps // block, combine, 0)
+
     def one_step(step, carry):
-        def fill(chunk, carry):
-            activate(step, chunk)
-            return carry
-
-        lax.fori_loop(0, chunks, fill, 0)
-
-        @pl.when(step == 0)
-        def _():
-            each_core(wait_all)
-            block = chans // 5
-
-            def combine(number, carry):
-                here = pl.multiple_of(number * block, block)
-                first, middle, final = (
-                    w_conv[pl.ds(tap * taps + here, block), :].astype(jnp.float32)
-                    for tap in range(3)
-                )
-                outer = 0.5 * (first + final)
-                w_plus[pl.ds(here, block), :] = (outer + 0.5 * middle).astype(jnp.bfloat16)
-                w_conv[pl.ds(taps + here, block), :] = (outer - 0.5 * middle).astype(
-                    jnp.bfloat16
-                )
-                return carry
-
-            lax.fori_loop(0, taps // block, combine, 0)
-
         lax.fori_loop(0, 2, convolve, 0)
         last = step == group - 1
         base = jnp.where(last, HALO, HALO // 2) * cols
+        count = jnp.where(last, chunks - 2, chunks - 1)
+        after = jnp.minimum(step + 1, group - 1)
+
+        def place(number):
+            return pl.multiple_of(base + number * size, 2 * cols)
 
         def rest(number, carry):
-            finish(step, pl.multiple_of(base + number * size, 2 * cols))
+            interleave(
+                finish(step, place(number)), activate(after, place(jnp.maximum(number - 1, 0)))
+            )
             return carry
 
-        lax.fori_loop(0, jnp.where(last, chunks - 2, chunks - 1), rest, 0)
+        lax.fori_loop(0, count, rest, 0)
+
+        @pl.when(step < group - 1)
+        def _():
+            interleave(activate(after, place(count - 1)))
+
         return carry
 
     lax.fori_loop(0, group, one_step, 0)
     x_out[...] = state[:, HALO * cols : (HALO + rows) * cols]
 
 
-def run_steps(rows, cols, counts, flags, factors, sources, x, noise, rest, bias):
+def run_steps(rows, cols, counts, split, relative, flags, factors, sources, x, noise, rest, bias):
     key_blocks, value_blocks, gains, w_in, w_final = rest
     feats, chans = w_in.shape
     tall_rows = rows + 2 * HALO
     vmem = pl.BlockSpec(memory_space=pltpu.VMEM)
     smem = pl.BlockSpec(memory_space=pltpu.SMEM)
     token_rows = sum(rows + 2 * k for k in range(GROUP)) * cols
-    most = sources[0].shape[0] * (1 if len(sources) == 1 else 2 * sources[0].shape[1])
+    most = sources[0].shape[0] + sum(len(places) for places in relative)
     return pl.pallas_call(
-        functools.partial(steps_kernel, rows, cols, counts, len(sources)),
+        functools.partial(steps_kernel, rows, cols, counts, split, relative),
         out_shape=(
             jax.ShapeDtypeStruct((feats, rows * cols), jnp.float32),
             jax.ShapeDtypeStruct((feats, chans), jnp.float32),
@@ -424,52 +437,59 @@
         w_final.astype(jnp.bfloat16).reshape(-1, col_piece),
     ]
     counts = [piece.shape[0] for piece in pieces]
+    big = counts[:3]
     used = sum(counts)
     unit = 16 * dev_count
     padded = -(-used // unit) * unit
+    whole_tiles = all(count % 16 == 0 for count in big)
+    doubled = int(padded * 0.36) // unit * unit if whole_tiles else 0
+    split = counts[0] - doubled
+    pieces = [w_conv[:split]] + pieces[1:]
     pieces.append(jnp.zeros((padded - used, col_piece), jnp.bfloat16))
-    block = jnp.concatenate(pieces, axis=0)
+    blocks = [jnp.concatenate(pieces, axis=0), w_conv[split:]]
+    main_length, length = (padded - doubled) // dev_count, doubled // dev_count
+    block = jnp.concatenate([b.reshape(dev_count, -1, col_piece) for b in blocks], axis=1)
+    block = block.reshape(padded, col_piece)
     block = lax.all_to_all(block, "dev", split_axis=0, concat_axis=1, tiled=True)
-    total = sec_count * dev_count
-    mates = [list(range(core, total, 2)) for core in range(2)]
-    mine = lax.all_gather(block, ("sec", "dev"), axis=0, tiled=True, axis_index_groups=mates)
-    theirs = swap(mine, "dev", 1)
-    core = lax.axis_index("dev") % 2
-    length = padded // dev_count
-    mine = mine.reshape(sec_count, dev_count // 2, length, chans)
-    theirs = theirs.reshape(mine.shape)
-
-    def rows_of(first, count, local):
-        if local and first // length == (first + count - 1) // length:
-            half, which = divmod(first // length, 2)
-            inner = slice(first % length, first % length + count)
-            return jnp.where(core == which, mine[:, half, inner], theirs[:, half, inner])
-        everything = jnp.where(
-            core == 0, jnp.stack([mine, theirs], axis=2), jnp.stack([theirs, mine], axis=2)
-        )
-        return everything.reshape(sec_count, padded, chans)[:, first : first + count]
-
-    at = counts[0] + counts[1] + counts[2]
-    small = rows_of(at, counts[3] + counts[4], True)
-    in_full = small[:, : counts[3]].reshape(feats, chans)
+    packed = lax.all_gather(block[:main_length], ("sec", "dev"), axis=0, tiled=True)
+    packed = packed.reshape(sec_count, padded - doubled, chans)
+    sources, relative = [packed], []
+    if doubled:
+        turns = [("dev", 1 << k) for k in range(1, dev_count.bit_length() - 1)]
+        turns += [("sec", 1 << k) for k in range(1, sec_count.bit_length() - 1)]
+        turns += [("sec", 1), ("dev", 1)]
+        held, places = [block[main_length:][None]], [((0, 0),)]
+        for number, (axis, mask) in enumerate(turns):
+            step = (mask, 0) if axis == "sec" else (0, mask)
+            new = [swap(piece, axis, mask) for piece in held]
+            new_places = [tuple((s ^ step[0], d ^ step[1]) for s, d in p) for p in places]
+            if number < len(turns) - 2:
+                held = [jnp.concatenate(held + new, axis=0)]
+                places = [places[0] + new_places[0]]
+            else:
+                held, places = held + new, places + new_places
+        sources, relative = sources + held, places
+
+    at = split + counts[1] + counts[2]
+    in_full = packed[:, at : at + counts[3]].reshape(feats, chans)
+    at += counts[3]
     final_full = (
-        small[:, counts[3] :]
+        packed[:, at : at + counts[4]]
         .reshape(sec_count, counts[4], dev_count, col_piece)
         .transpose(0, 2, 1, 3)
         .reshape(sec_count, dev_count, chans // sec_count, feats // dev_count)
         .transpose(0, 2, 1, 3)
         .reshape(chans, feats)
     )
-    big = counts[:3]
-    sources = (mine, theirs)
-    if any(count % 16 for count in big):
+    if not whole_tiles:
         first = [sum(big[:k]) for k in range(3)]
-        sources = (
+        sources = [
             jnp.concatenate(
-                [rows_of(f, c, False).reshape(-1, chans) for f, c in zip(first, big)], axis=0
-            )[None],
-        )
+                [packed[:, f : f + c].reshape(-1, chans) for f, c in zip(first, big)], axis=0
+            )[None]
+        ]
         big = [count * sec_count for count in big]
+        split = big[0]
 
     both = jnp.stack([rewards, prompt_ids.astype(jnp.float32)], axis=1)
     both = doubled_gather(both, "sec")
@@ -520,14 +540,16 @@
     )
 
     position = lax.axis_index("dev")
-    flags = jnp.stack([position > 0, position < dev_count - 1, core == 1]).astype(jnp.int32)
+    flags = jnp.stack(
+        [position > 0, position < dev_count - 1, lax.axis_index("sec"), position]
+    ).astype(jnp.int32)
     planes = jnp.concatenate([latents, noise[:, 0]], axis=0)
     planes = to_tokens(with_halo(planes, "dev", 2, 2 * HALO))
     x, noise_wide = planes[0], planes[1:]
     plans = [plan(k) for k in range(STEPS)]
     factors = jnp.array([(s, b, g, b / g) for s, b, g in plans], jnp.float32)
 
-    gains = jnp.stack([gain_first, gain_second, gain_third])
+    gains = jnp.stack([0.5 * gain_first, gain_second, 0.5 * gain_third])
     rest = (key_blocks, value_blocks, gains, in_full, final_full)
     gradient = jnp.zeros((feats, chans), jnp.float32)
     for first in range(0, STEPS, GROUP):
@@ -538,6 +560,8 @@
             rows,
             cols,
             big,
+            split,
+            relative,
             flags,
             factors[part],
             sources,
@@ -552,7 +576,7 @@
     gradient = gradient * advantage
     row_piece = chans // sec_count
     arranged = gradient.reshape(dev_count, feats // dev_count, sec_count, row_piece)
-    arranged = arranged.transpose(2, 0, 1, 3).reshape(total, -1)
+    arranged = arranged.transpose(2, 0, 1, 3).reshape(sec_count * dev_count, -1)
     arrived = lax.all_to_all(arranged, ("sec", "dev"), split_axis=0, concat_axis=0, tiled=True)
     grad_shard = jnp.sum(arrived, axis=0).reshape(feats // dev_count, row_piece).T
     grad_shard = -grad_shard / sec_count

time: 304 us -> 289 us (0.951)
  waiting for transfers between devices: 95.3 us -> 72.5 us
  starting transfers between devices: 22.5 us -> 30.7 us
  Pallas kernels: 130 us -> 126 us
    all_gather x1, waiting for transfers between devices: 62 us -> 0.02 us  [per_device(): lax.all_gather(block[:main_length], ('sec', 'dev'), axis=0, tiled=True)]
    ppermute x9 -> x14, waiting for transfers between devices: 27.1 us -> 66.3 us  [swap(): return lax.ppermute(value, axis, [(i, i ^ mask) for i in range(size)])]
    ppermute x9 -> x14, starting transfers between devices: 11 us -> 18.9 us  [swap(): return lax.ppermute(value, axis, [(i, i ^ mask) for i in range(size)])]
    pallas_call x2, Pallas kernels: 130 us -> 126 us  [run_steps(): pl.pallas_call(functools.partial(steps_kernel, rows, cols, counts, split,...]
    slice x1 -> x5, local copies, waits for them, and re-layouts: 0.03 us -> 3.96 us  [the longest x1 1.09 us: per_device(): blocks = [jnp.concatenate(pieces, axis=0), w_conv[split:]]]
    concatenate x0 -> x4, other arithmetic: none -> 3.21 us  [the longest x3 2.92 us: per_device(): held = [jnp.concatenate(held + new, axis=0)]]
  transfers between devices with their start and end apart: 15 -> 20, of which waited for: 8 -> 11; matrix products, arithmetic and copies ran while one was open for 6% -> 7% of each run, Pallas kernels for 0% -> 0%
where the time goes in v2:
time: 289 us
  Pallas kernels  126 us (44%)
  waiting for transfers between devices  72.5 us (25%)
  starting transfers between devices  30.7 us (11%)
  between operations  17.5 us (6%)
  local copies, waits for them, and re-layouts  17.4 us (6%)
  blocking collectives  10.7 us (4%)
  other arithmetic  10.2 us (4%)
  matrix products  3.28 us (1%)
    pallas_call x2, Pallas kernels, run_steps(): pl.pallas_call(functools.partial(steps_kernel, rows, cols, counts, split,...  126 us
    ppermute x14, waiting for transfers between devices, swap(): return lax.ppermute(value, axis, [(i, i ^ mask) for i in range(size)])  66.3 us
    ppermute x14, starting transfers between devices, swap(): return lax.ppermute(value, axis, [(i, i ^ mask) for i in range(size)])  18.9 us
    all_to_all x1, blocking collectives, per_device(): lax.all_to_all(block, 'dev', split_axis=0, concat_axis=1, tiled=True)  10.7 us
    all_to_all x1, waiting for transfers between devices, per_device(): lax.all_to_all(arranged, ('sec', 'dev'), split_axis=0, concat_axis=0, til...  6.2 us
  transfers between devices with their start and end apart: 20, of which 11 were waited for; matrix products, arithmetic and copies ran while one was open for 7% of the time, Pallas kernels for 0%

profile of v2, /device:TPU:0, one launch (start us, length us, event | category | flops | bytes accessed | tf_op | source)
XLA Modules:
  0.0 288.6 jit_solution(5198853243994914562)
XLA Ops:
  13.9 10.7 %all_to_all.23 = bf16[4,224,160]{1,2,0:T(8,128)(2,1)S(1)} all-to-all(bf16[4,224,160]{1,2,0:T(8,128)(2,1)S(1)} %copy.77), channel_id=1, replica_groups=mesh['sec'=8,'dev'=4] {'dev'}, dimensions={0} | all-to-all | bytes 573440 | tf_op jit(solution)/shard_map/all_to_all | solution.py:453
  26.9 1.6 collective-permute-start.8
  28.5 2.0 collective-permute-start.6
  34.5 1.6 collective-permute-start.9
  36.1 2.0 collective-permute-done.9
  38.3 2.6 collective-permute-start.10
  40.9 1.9 collective-permute-done.10
  43.9 2.7 collective-permute-start.11
  46.6 15.6 %collective-permute-done.11 = bf16[4,80,320]{2,0,1:T(4,128)(2,1)S(1)} collective-permute-done((bf16[4,80,320]{2,0,1:T(4,128)(2,1)S(1)}, bf16[4,80,320]{2,0,1:T(4,128)(2,1)S(1)}, u32[]{:S(2)}, u32[]{:S(2)}) %collective-permute-start.11) | collective-permute-done | bytes 204832 | tf_op jit(solution)/shard_map/ppermute | solution.py:33
  62.6 2.7 collective-permute-start.12
  65.7 2.0 collective-permute-start
  70.8 3.2 %collective-permute-done.13 = bf16[1,80,320]{2,0,1:T(2,128)(2,1)S(1)} collective-permute-done((bf16[1,80,320]{2,0,1:T(2,128)(2,1)S(1)}, bf16[1,80,320]{2,0,1:T(2,128)(2,1)S(1)}, u32[]{:S(2)}, u32[]{:S(2)}) %collective-permute-start.13) | collective-permute-done | bytes 51232 | tf_op jit(solution)/shard_map/ppermute | solution.py:33
  74.8 10.0 %collective-permute-done.1 = bf16[2,80,640]{2,1,0:T(8,128)(2,1)S(1)} collective-permute-done((bf16[2,80,640]{2,1,0:T(8,128)(2,1)S(1)}, bf16[2,80,640]{2,1,0:T(8,128)(2,1)S(1)}, u32[]{:S(2)}, u32[]{:S(2)}) %collective-permute-start.1) | collective-permute-done | bytes 204832 | tf_op jit(solution)/shard_map/ppermute | solution.py:33
  85.7 1.9 collective-permute-start.2
  87.6 1.4 fusion
  91.5 1.8 collective-permute-start.15
  93.3 17.3 %collective-permute-done.2 = bf16[4,80,640]{2,1,0:T(8,128)(2,1)} collective-permute-done((bf16[4,80,640]{2,1,0:T(8,128)(2,1)}, bf16[4,80,640]{2,1,0:T(8,128)(2,1)}, u32[]{:S(2)}, u32[]{:S(2)}) %collective-permute-start.2) | collective-permute-done | bytes 409632 | tf_op jit(solution)/shard_map/ppermute | solution.py:33
  110.6 2.0 pad_maximum_fusion.refs_1_
  118.0 13.9 %collective-permute-done.3.refs_2_ = bf16[8,80,640]{2,1,0:T(8,128)(2,1)} collective-permute-done((bf16[8,80,640]{2,1,0:T(8,128)(2,1)}, bf16[8,80,640]{2,1,0:T(8,128)(2,1)}, u32[]{:S(2)}, u32[]{:S(2)}) %collective-permute-start.3) | collective-permute-done | bytes 819232 | tf_op jit(solution)/shard_map/ppermute | solution.py:33
  134.6 63.0 %shard_map.210 = (f32[16,1024]{1,0:T(8,128)S(1)}, f32[16,640]{1,0:T(8,128)S(1)}) custom-call(s32[4]{0:T(128)S(1)} %pad_add_fusion.flags, f32[3,4]{1,0:T(4,128)S(1)} %copy-done.2, bf16[8,576,640]{2,1,0:T(8,128)(2,1)} %bitcast.127, bf16[8,80,640]{2,1,0:T(8,128)(2,1)} %pad_maximum_fusion.refs_1_, bf16[8,80,640]{2,1,0:T(8,128)(2,1)} %collective-permute-done.3.refs_2_, ...), custom_call_target="tpu_custom_call" | custom-call | flops 33973862400 | bytes 9830400 | tf_op jit(solution)/shard_map/pallas_call | solution.py:362
  197.6 2.1 collective-permute-start.16
  204.2 63.2 %shard_map.211 = (f32[16,1024]{1,0:T(8,128)S(1)}, f32[16,640]{1,0:T(8,128)S(1)}) custom-call(s32[4]{0:T(128)S(1)} %pad_add_fusion.flags, f32[3,4]{1,0:T(4,128)S(1)} %copy-done.1, bf16[8,576,640]{2,1,0:T(8,128)(2,1)} %bitcast.128, bf16[8,80,640]{2,1,0:T(8,128)(2,1)} %pad_maximum_fusion.refs_1_, bf16[8,80,640]{2,1,0:T(8,128)(2,1)} %collective-permute-done.3.refs_2_, ...), custom_call_target="tpu_custom_call" | custom-call | flops 33973862400 | bytes 9830400 | tf_op jit(solution)/shard_map/pallas_call | solution.py:362
  268.4 5.1 %all-to-all-start.1 = ((f32[32,1,320]{2,1,0:T(1,128)}), f32[32,1,320]{2,1,0:T(1,128)S(1)}, u32[]{:S(2)}, u32[]{:S(2)}) async-start(f32[32,1,320]{2,1,0:T(1,128)} %all_to_all.20), calls=%async_computation.1 | async-start | bytes 98304 | tf_op jit(solution)/shard_map/all_to_all | solution.py:580
  274.7 6.2 %all-to-all-done.1 = f32[32,1,320]{2,1,0:T(1,128)S(1)} async-done(((f32[32,1,320]{2,1,0:T(1,128)}), f32[32,1,320]{2,1,0:T(1,128)S(1)}, u32[]{:S(2)}, u32[]{:S(2)}) %all-to-all-start.1) | async-done | bytes 40992 | tf_op jit(solution)/shard_map/all_to_all | solution.py:580
  (173 shorter events, 34.5 us)
Async XLA Ops:
  7.2 26.8 %copy-start = (bf16[4,77,2048]{2,0,1:T(4,128)(2,1)S(1)}, bf16[4,77,2048]{2,0,1:T(4,128)(2,1)}, u32[]{:S(2)}) copy-start(bf16[4,77,2048]{2,0,1:T(4,128)(2,1)} %param.23) | copy-start | bytes 3784708
  7.2 125.0 %all-gather.2.cloned.1.call-start = ((), (), s32[]{:S(2)}) async-start(), calls=%async_computation.2 | async-start | bytes 6082560 | tf_op jit(solution)/shard_map/all_gather | solution.py:454
  26.9 7.5 %collective-permute-start.8 = (f32[1,2]{0,1:T(2,128)S(1)}, f32[1,2]{0,1:T(2,128)S(1)}, u32[]{:S(2)}, u32[]{:S(2)}) collective-permute-start(f32[1,2]{0,1:T(2,128)S(1)} %pad_maximum_fusion.11), channel_id=1, source_target_pairs={{0,4},{4,0},{8,12},{12,8},{16,20},{20,16},{24,28},{28,24},{1,5},{5... | collective-permute-start | bytes 32 | tf_op jit(solution)/shard_map/ppermute | solution.py:33
  28.5 59.1 %collective-permute-start.6 = (f32[7,4,8,128]{3,2,1,0:T(8,128)S(1)}, f32[7,4,8,128]{3,2,1,0:T(8,128)}, u32[]{:S(2)}, u32[]{:S(2)}) collective-permute-start(f32[7,4,8,128]{3,2,1,0:T(8,128)S(1)} %get-tuple-element.24), channel_id=1, source_target_pairs={{0,1},{1,2},{2,3},{4,5},{5,6},{6,7},{8,9},{9,10},{10,11},{12,13},{... | collective-permute-start | bytes 344072 | tf_op jit(solution)/shard_map/ppermute | solution.py:70
  30.5 57.1 %collective-permute-start.7 = (f32[7,4,8,128]{3,2,1,0:T(8,128)S(1)}, f32[7,4,8,128]{3,2,1,0:T(8,128)}, u32[]{:S(2)}, u32[]{:S(2)}) collective-permute-start(f32[7,4,8,128]{3,2,1,0:T(8,128)S(1)} %get-tuple-element.25), channel_id=1, source_target_pairs={{1,0},{2,1},{3,2},{5,4},{6,5},{7,6},{9,8},{10,9},{11,10},{13,12},{... | collective-permute-start | bytes 344072 | tf_op jit(solution)/shard_map/ppermute | solution.py:71
  34.5 3.6 %collective-permute-start.9 = (f32[2,2]{0,1:T(2,128)S(1)}, f32[2,2]{0,1:T(2,128)S(1)}, u32[]{:S(2)}, u32[]{:S(2)}) collective-permute-start(f32[2,2]{0,1:T(2,128)S(1)} %pad_maximum_fusion.12), channel_id=1, source_target_pairs={{0,8},{4,12},{8,0},{12,4},{16,24},{20,28},{24,16},{28,20},{1,9},{5... | collective-permute-start | bytes 56 | tf_op jit(solution)/shard_map/ppermute | solution.py:33
  38.3 4.5 %collective-permute-start.10 = (f32[4,2]{0,1:T(2,128)S(1)}, f32[4,2]{0,1:T(2,128)S(1)}, u32[]{:S(2)}, u32[]{:S(2)}) collective-permute-start(f32[4,2]{0,1:T(2,128)S(1)} %pad_maximum_fusion.13), channel_id=1, source_target_pairs={{0,16},{4,20},{8,24},{12,28},{16,0},{20,4},{24,8},{28,12},{1,17},{... | collective-permute-start | bytes 104 | tf_op jit(solution)/shard_map/ppermute | solution.py:33
  43.9 18.3 %collective-permute-start.11 = (bf16[4,80,320]{2,0,1:T(4,128)(2,1)S(1)}, bf16[4,80,320]{2,0,1:T(4,128)(2,1)S(1)}, u32[]{:S(2)}, u32[]{:S(2)}) collective-permute-start(bf16[4,80,320]{2,0,1:T(4,128)(2,1)S(1)} %select_convert_fusion), channel_id=1, source_target_pairs={{0,16},{4,20},{8,24},{12,28},{16,0},{20,4},{24,8},{28,12},{1,17},{... | collective-permute-start | bytes 614408 | tf_op jit(solution)/shard_map/ppermute | solution.py:33
  62.6 6.1 %collective-permute-start.12 = (bf16[2,80,320]{2,0,1:T(2,128)(2,1)S(1)}, bf16[2,80,320]{2,0,1:T(2,128)(2,1)S(1)}, u32[]{:S(2)}, u32[]{:S(2)}) collective-permute-start(bf16[2,80,320]{2,0,1:T(2,128)(2,1)S(1)} %select_convert_fusion.1), channel_id=1, source_target_pairs={{0,8},{4,12},{8,0},{12,4},{16,24},{20,28},{24,16},{28,20},{1,9},{5... | collective-permute-start | bytes 307208 | tf_op jit(solution)/shard_map/ppermute | solution.py:33
  65.7 21.9 %copy-start.9 = (f32[1,4,32,128]{3,2,1,0:T(8,128)S(1)}, f32[1,4,32,128]{3,2,1,0:T(8,128)}, u32[]{:S(2)}) copy-start(f32[1,4,32,128]{3,2,1,0:T(8,128)} %param.19) | copy-start | bytes 196612
  65.7 4.7 %collective-permute-start = (bf16[1,80,640]{2,1,0:T(8,128)(2,1)S(1)}, bf16[1,80,640]{2,1,0:T(8,128)(2,1)S(1)}, u32[]{:S(2)}, u32[]{:S(2)}) collective-permute-start(bf16[1,80,640]{2,1,0:T(8,128)(2,1)S(1)} %copy.98), channel_id=1, source_target_pairs={{0,2},{1,3},{2,0},{3,1},{4,6},{5,7},{6,4},{7,5},{8,10},{9,11},{10,... | collective-permute-start | bytes 307208 | tf_op jit(solution)/shard_map/ppermute | solution.py:33
  69.0 4.9 %collective-permute-start.13 = (bf16[1,80,320]{2,0,1:T(2,128)(2,1)S(1)}, bf16[1,80,320]{2,0,1:T(2,128)(2,1)S(1)}, u32[]{:S(2)}, u32[]{:S(2)}) collective-permute-start(bf16[1,80,320]{2,0,1:T(2,128)(2,1)S(1)} %fusion.19), channel_id=1, source_target_pairs={{0,4},{4,0},{8,12},{12,8},{16,20},{20,16},{24,28},{28,24},{1,5},{5... | collective-permute-start | bytes 153608 | tf_op jit(solution)/shard_map/ppermute | solution.py:33
  70.5 14.4 %collective-permute-start.1 = (bf16[2,80,640]{2,1,0:T(8,128)(2,1)S(1)}, bf16[2,80,640]{2,1,0:T(8,128)(2,1)S(1)}, u32[]{:S(2)}, u32[]{:S(2)}) collective-permute-start(bf16[2,80,640]{2,1,0:T(8,128)(2,1)S(1)} %pad_maximum_fusion.5), channel_id=1, source_target_pairs={{0,8},{4,12},{8,0},{12,4},{16,24},{20,28},{24,16},{28,20},{1,9},{5... | collective-permute-start | bytes 614408 | tf_op jit(solution)/shard_map/ppermute | solution.py:33
  74.8 15.1 %collective-permute-start.14 = (bf16[1,80,320]{2,0,1:T(2,128)(2,1)}, bf16[1,80,320]{2,0,1:T(2,128)(2,1)}, u32[]{:S(2)}, u32[]{:S(2)}) collective-permute-start(bf16[1,80,320]{2,0,1:T(2,128)(2,1)} %fusion.18), channel_id=1, source_target_pairs={{0,1},{1,0},{2,3},{3,2},{4,5},{5,4},{6,7},{7,6},{8,9},{9,8},{10,11... | collective-permute-start | bytes 153608 | tf_op jit(solution)/shard_map/ppermute | solution.py:33
  85.7 24.9 %collective-permute-start.2 = (bf16[4,80,640]{2,1,0:T(8,128)(2,1)}, bf16[4,80,640]{2,1,0:T(8,128)(2,1)}, u32[]{:S(2)}, u32[]{:S(2)}) collective-permute-start(bf16[4,80,640]{2,1,0:T(8,128)(2,1)} %pad_maximum_fusion.2), channel_id=1, source_target_pairs={{0,16},{4,20},{8,24},{12,28},{16,0},{20,4},{24,8},{28,12},{1,17},{... | collective-permute-start | bytes 1228808 | tf_op jit(solution)/shard_map/ppermute | solution.py:33
  89.8 20.8 %copy-start.5 = (bf16[1,80,640]{2,1,0:T(8,128)(2,1)S(1)}, bf16[1,80,640]{2,1,0:T(8,128)(2,1)}, u32[]{:S(2)}) copy-start(bf16[1,80,640]{2,1,0:T(8,128)(2,1)} %copy-done.4) | copy-start | bytes 307204
  91.5 23.4 %collective-permute-start.15 = (bf16[2,80,320]{2,0,1:T(2,128)(2,1)S(1)}, bf16[2,80,320]{2,0,1:T(2,128)(2,1)S(1)}, u32[]{:S(2)}, u32[]{:S(2)}) collective-permute-start(bf16[2,80,320]{2,0,1:T(2,128)(2,1)S(1)} %pad_maximum_fusion.6), channel_id=1, source_target_pairs={{0,2},{1,3},{2,0},{3,1},{4,6},{5,7},{6,4},{7,5},{8,10},{9,11},{10,... | collective-permute-start | bytes 307208 | tf_op jit(solution)/shard_map/ppermute | solution.py:33
  112.7 19.3 %collective-permute-start.3 = (bf16[8,80,640]{2,1,0:T(8,128)(2,1)}, bf16[8,80,640]{2,1,0:T(8,128)(2,1)}, u32[]{:S(2)}, u32[]{:S(2)}) collective-permute-start(bf16[8,80,640]{2,1,0:T(8,128)(2,1)} %pad_maximum_fusion.refs_1_), channel_id=1, source_target_pairs={{0,4},{4,0},{8,12},{12,8},{16,20},{20,16},{24,28},{28,24},{1,5},{5... | collective-permute-start | bytes 2457608 | tf_op jit(solution)/shard_map/ppermute | solution.py:33
  117.9 16.1 %collective-permute-start.4 = (bf16[8,80,640]{2,1,0:T(8,128)(2,1)}, bf16[8,80,640]{2,1,0:T(8,128)(2,1)}, u32[]{:S(2)}, u32[]{:S(2)}) collective-permute-start(bf16[8,80,640]{2,1,0:T(8,128)(2,1)} %pad_maximum_fusion.refs_1_), channel_id=1, source_target_pairs={{0,1},{1,0},{2,3},{3,2},{4,5},{5,4},{6,7},{7,6},{8,9},{9,8},{10,11... | collective-permute-start | bytes 2457608 | tf_op jit(solution)/shard_map/ppermute | solution.py:33
  131.9 2.7 collective-permute-start.5
  134.6 69.6 %copy-start.1 = (f32[3,4]{1,0:T(4,128)S(1)}, f32[3,4]{1,0:T(4,128)}, u32[]{:S(2)}) copy-start(f32[3,4]{1,0:T(4,128)} %constant.104.factors) | copy-start | bytes 148
  197.6 6.6 %collective-permute-start.16 = (f32[16,256]{1,0:T(8,128)S(1)}, f32[16,256]{1,0:T(8,128)S(1)}, u32[]{:S(2)}, u32[]{:S(2)}) collective-permute-start(f32[16,256]{1,0:T(8,128)S(1)} %get-tuple-element.32), channel_id=1, source_target_pairs={{0,1},{1,2},{2,3},{4,5},{5,6},{6,7},{8,9},{9,10},{10,11},{12,13},{... | collective-permute-start | bytes 49160 | tf_op jit(solution)/shard_map/ppermute | solution.py:70
  199.7 4.5 %collective-permute-start.17 = (f32[16,256]{1,0:T(8,128)S(1)}, f32[16,256]{1,0:T(8,128)S(1)}, u32[]{:S(2)}, u32[]{:S(2)}) collective-permute-start(f32[16,256]{1,0:T(8,128)S(1)} %get-tuple-element.33), channel_id=1, source_target_pairs={{1,0},{2,1},{3,2},{5,4},{6,5},{7,6},{9,8},{10,9},{11,10},{13,12},{... | collective-permute-start | bytes 49160 | tf_op jit(solution)/shard_map/ppermute | solution.py:71
  268.4 12.5 %all-to-all-start.1 = ((f32[32,1,320]{2,1,0:T(1,128)}), f32[32,1,320]{2,1,0:T(1,128)S(1)}, u32[]{:S(2)}, u32[]{:S(2)}) async-start(f32[32,1,320]{2,1,0:T(1,128)} %all_to_all.20), calls=%async_computation.1 | async-start | bytes 98304 | tf_op jit(solution)/shard_map/all_to_all | solution.py:580
  (17 other events, 227.4 us)
Sparse Core Ops, SparseCore 0:
  25.7 82.0 all-gather.1

commit v3 on v2

--- a/solution.py
+++ b/solution.py
@@ -10,6 +10,7 @@
 
 HEAD = 64
 STEPS = 6
+LANES = 128
 GROUP = 3
 HALO = 4
 CHUNK_ROWS = 4
@@ -46,18 +47,6 @@
             [jnp.where(upper, other, value), jnp.where(upper, value, other)], axis=0
         )
         mask *= 2
-    return value
-
-
-def halved_sum(value, axis, link=jnp.float32):
-    mask = lax.axis_size(axis) // 2
-    while mask >= 1:
-        half = value.shape[0] // 2
-        upper = bit_of(axis, mask)
-        kept = jnp.where(upper, value[half:], value[:half])
-        sent = jnp.where(upper, value[:half], value[half:])
-        value = kept + swap(sent.astype(link), axis, mask).astype(value.dtype)
-        mask //= 2
     return value
 
 
@@ -173,6 +162,10 @@
         hidden,
         columns,
         state,
+        narrow,
+        queries,
+        added,
+        acts,
         sems,
     ) = refs[source_count:]
     group = bias.shape[0]
@@ -193,8 +186,8 @@
     near = lax.broadcasted_iota(jnp.int32, (edge, 1), 0)
     taps = 3 * chans
 
-    def activate(step, start):
-        before_norm = (
+    def activate(step, start, first):
+        hidden[pl.ds(first, CHUNK_ROWS // 2)] = (
             lax.dot_general(
                 state[:, pl.ds(start, size)].astype(jnp.bfloat16),
                 w_in[...],
@@ -202,32 +195,37 @@
                 preferred_element_type=jnp.float32,
             )
             + bias[pl.ds(step, 1), :]
-        )
-        first = lax.div(start, 2 * cols)
+        ).reshape(CHUNK_ROWS // 2, 2, cols, chans)
         yield
         for row in range(CHUNK_ROWS):
-            value = before_norm[row * cols : (row + 1) * cols]
-            hidden[first + row // 2, row % 2] = value
-            act = silu_of_twice(rms_scale(value, gains[0:1, :]))
             place = 2 * first + row
             inside = jnp.where(
                 place < HALO, flags[0], jnp.where(place >= HALO + rows, flags[1], 1)
-            )
-            act = act * inside.astype(jnp.float32)
+            ).astype(jnp.float32)
+            scales = []
+            for low in range(0, cols, edge):
+                value = hidden[first + row // 2, row % 2, low : low + edge, :]
+                mean_square = jnp.mean(value * value, axis=-1, keepdims=True)
+                scales.append(lax.rsqrt(mean_square + norm_eps))
+            scales = jnp.concatenate(scales, axis=0)
             at = (first + (row + 1) // 2, (row + 1) % 2)
-            left = pltpu.roll(act, 1, 0)
-            right = pltpu.roll(act, cols - 1, 0)
-            first_left = jnp.where(near == 0, 0.0, left[:edge])
-            last_right = jnp.where(near == edge - 1, 0.0, right[cols - edge :])
-            columns[at + (slice(0, edge), slice(0, chans))] = first_left.astype(jnp.bfloat16)
-            columns[at + (slice(edge, cols), slice(0, chans))] = left[edge:].astype(jnp.bfloat16)
-            columns[at + (slice(0, cols), slice(chans, 2 * chans))] = act.astype(jnp.bfloat16)
-            columns[at + (slice(0, cols - edge), slice(2 * chans, taps))] = right[
-                : cols - edge
-            ].astype(jnp.bfloat16)
-            columns[at + (slice(cols - edge, cols), slice(2 * chans, taps))] = last_right.astype(
-                jnp.bfloat16
-            )
+            for low in range(0, chans, LANES):
+                lanes = slice(low, low + LANES)
+                value = hidden[first + row // 2, row % 2, :, lanes]
+                act = silu_of_twice(value * scales * gains[0:1, lanes]) * inside
+                left = pltpu.roll(act, 1, 0)
+                right = pltpu.roll(act, cols - 1, 0)
+                left = jnp.concatenate(
+                    [jnp.where(near == 0, 0.0, left[:edge]), left[edge:]], axis=0
+                )
+                right = jnp.concatenate(
+                    [right[: cols - edge], jnp.where(near == edge - 1, 0.0, right[cols - edge :])],
+                    axis=0,
+                )
+                for which, piece in enumerate((left, act, right)):
+                    columns[
+                        at + (slice(None), pl.ds(which * chans + low, LANES))
+                    ] = piece.astype(jnp.bfloat16)
             yield
 
     twos = (rows + HALO) // 4
@@ -253,35 +251,41 @@
 
     def finish(step, start):
         row_pair = lax.div(start, 2 * cols)
-        mixed = hidden[pl.ds(row_pair, CHUNK_ROWS // 2)].reshape(size, chans)
-        normed = rms_scale(mixed, gains[1:2, :]).astype(jnp.bfloat16)
+
+        def mixed_block(low):
+            row = low // cols
+            return hidden[row_pair + row // 2, row % 2, low % cols : low % cols + edge, :]
+
+        for low in range(0, size, edge):
+            value = rms_scale(mixed_block(low), gains[1:2, :])
+            narrow[low : low + edge, :] = value.astype(jnp.bfloat16)
         yield
-        queries = jnp.dot(normed, w_query[...], preferred_element_type=jnp.float32).astype(
-            jnp.bfloat16
-        )
+        queries[...] = jnp.dot(
+            narrow[...], w_query[...], preferred_element_type=jnp.float32
+        ).astype(jnp.bfloat16)
         yield
-        heads = []
         for pair in range(pairs):
+            lanes = slice(pair * wide, (pair + 1) * wide)
             scores = jnp.dot(
-                queries[:, pair * wide : (pair + 1) * wide],
-                key_blocks[pair],
-                preferred_element_type=jnp.float32,
+                queries[:, lanes], key_blocks[pair], preferred_element_type=jnp.float32
             )
             sums = jnp.dot(
                 jnp.exp(scores).astype(jnp.bfloat16),
                 value_blocks[pair],
                 preferred_element_type=jnp.float32,
             )
-            heads.append(
-                (sums[:, :wide] * pl.reciprocal(sums[:, wide:], approx=True)).astype(
-                    jnp.bfloat16
-                )
-            )
+            narrow[:, lanes] = (
+                sums[:, :wide] * pl.reciprocal(sums[:, wide:], approx=True)
+            ).astype(jnp.bfloat16)
             yield
-        attended = jnp.concatenate(heads, axis=1)
-        output = mixed + jnp.dot(attended, w_attn[...], preferred_element_type=jnp.float32)
-        act = silu_of_twice(rms_scale(output, gains[2:3, :])).astype(jnp.bfloat16)
-        predicted = jnp.dot(act, w_final[...], preferred_element_type=jnp.float32)
+        added[...] = jnp.dot(narrow[...], w_attn[...], preferred_element_type=jnp.float32)
+        yield
+        for low in range(0, size, edge):
+            output = mixed_block(low) + added[low : low + edge, :]
+            act = silu_of_twice(rms_scale(output, gains[2:3, :]))
+            acts[low : low + edge, :] = act.astype(jnp.bfloat16)
+        yield
+        predicted = jnp.dot(acts[...], w_final[...], preferred_element_type=jnp.float32)
         span = pl.ds(start, size)
         noise_now = noise[step, :, span]
         state[:, span] = (
@@ -295,14 +299,14 @@
         upper = weights.astype(jnp.bfloat16)
         lower = (weights - upper.astype(jnp.float32)).astype(jnp.bfloat16)
         share = jnp.dot(
-            jnp.concatenate([upper, lower], axis=0), act, preferred_element_type=jnp.float32
+            jnp.concatenate([upper, lower], axis=0), acts[...], preferred_element_type=jnp.float32
         )
         grad_out[...] += factors[step, 3] * (share[:feats] + share[feats:])
 
     chunks = state.shape[1] // size
 
     def fill(chunk, carry):
-        interleave(activate(0, pl.multiple_of(chunk * size, size)))
+        interleave(activate(0, pl.multiple_of(chunk * size, size), chunk * (CHUNK_ROWS // 2)))
         return carry
 
     lax.fori_loop(0, chunks, fill, 0)
@@ -334,16 +338,17 @@
             return pl.multiple_of(base + number * size, 2 * cols)
 
         def rest(number, carry):
-            interleave(
-                finish(step, place(number)), activate(after, place(jnp.maximum(number - 1, 0)))
-            )
+            start = place(jnp.maximum(number - 1, 0))
+            first = jnp.where(number == 0, state.shape[1] // (2 * cols), lax.div(start, 2 * cols))
+            interleave(finish(step, place(number)), activate(after, start, first))
             return carry
 
         lax.fori_loop(0, count, rest, 0)
 
         @pl.when(step < group - 1)
         def _():
-            interleave(activate(after, place(count - 1)))
+            start = place(count - 1)
+            interleave(activate(after, start, lax.div(start, 2 * cols)))
 
         return carry
 
@@ -374,9 +379,13 @@
             pltpu.VMEM((3 * chans, chans), jnp.bfloat16),
             pltpu.VMEM((chans, chans), jnp.bfloat16),
             pltpu.VMEM((chans, chans), jnp.bfloat16),
-            pltpu.VMEM((tall_rows // 2, 2, cols, chans), jnp.float32),
-            pltpu.VMEM((tall_rows // 2 + 1, 2, cols, 3 * chans), jnp.bfloat16),
+            pltpu.VMEM(((tall_rows + CHUNK_ROWS) // 2, 2, cols, chans), jnp.float32),
+            pltpu.VMEM(((tall_rows + CHUNK_ROWS) // 2 + 1, 2, cols, 3 * chans), jnp.bfloat16),
             pltpu.VMEM((feats, tall_rows * cols), jnp.float32),
+            pltpu.VMEM((CHUNK_ROWS * cols, chans), jnp.bfloat16),
+            pltpu.VMEM((CHUNK_ROWS * cols, chans), jnp.bfloat16),
+            pltpu.VMEM((CHUNK_ROWS * cols, chans), jnp.float32),
+            pltpu.VMEM((CHUNK_ROWS * cols, chans), jnp.bfloat16),
             pltpu.SemaphoreType.DMA((3, most)),
         ],
         compiler_params=pltpu.CompilerParams(vmem_limit_bytes=52 * 2**20),
@@ -454,6 +463,7 @@
     packed = lax.all_gather(block[:main_length], ("sec", "dev"), axis=0, tiled=True)
     packed = packed.reshape(sec_count, padded - doubled, chans)
     sources, relative = [packed], []
+    after = [jnp.float32(0), jnp.float32(0)]
     if doubled:
         turns = [("dev", 1 << k) for k in range(1, dev_count.bit_length() - 1)]
         turns += [("sec", 1 << k) for k in range(1, sec_count.bit_length() - 1)]
@@ -463,6 +473,8 @@
             step = (mask, 0) if axis == "sec" else (0, mask)
             new = [swap(piece, axis, mask) for piece in held]
             new_places = [tuple((s ^ step[0], d ^ step[1]) for s, d in p) for p in places]
+            if number < 2:
+                after[number] = (new[0][0, 0, 0] * 0).astype(jnp.float32)
             if number < len(turns) - 2:
                 held = [jnp.concatenate(held + new, axis=0)]
                 places = [places[0] + new_places[0]]
@@ -491,7 +503,7 @@
         big = [count * sec_count for count in big]
         split = big[0]
 
-    both = jnp.stack([rewards, prompt_ids.astype(jnp.float32)], axis=1)
+    both = jnp.stack([rewards, prompt_ids.astype(jnp.float32)], axis=1) + after[0]
     both = doubled_gather(both, "sec")
     all_rewards = both[:, 0]
     catalog = jnp.arange(prompt_count, dtype=jnp.int32)
@@ -511,9 +523,10 @@
         preferred_element_type=jnp.float32,
     ).reshape(prompt_count, tokens_up, 2 * col_piece)
     wanted = jnp.einsum(
-        "ip,ptc->itc", onehot, partial, precision=lax.Precision.HIGHEST
-    )
-    own_part = halved_sum(wanted, "sec", jnp.bfloat16).astype(jnp.bfloat16)
+        "ip,ptc->itc", onehot + after[1], partial, precision=lax.Precision.HIGHEST
+    ).astype(jnp.bfloat16)
+    arrived = lax.all_to_all(wanted, "sec", split_axis=0, concat_axis=0, tiled=True)
+    own_part = jnp.sum(arrived.astype(jnp.float32), axis=0, keepdims=True).astype(jnp.bfloat16)
     whole = doubled_gather(own_part, "dev").reshape(dev_count, tokens_up, 2, col_piece)
     whole = whole.transpose(2, 1, 0, 3).reshape(2, tokens_up, chans)
     lane = 2 * HEAD
@@ -543,7 +556,7 @@
     flags = jnp.stack(
         [position > 0, position < dev_count - 1, lax.axis_index("sec"), position]
     ).astype(jnp.int32)
-    planes = jnp.concatenate([latents, noise[:, 0]], axis=0)
+    planes = jnp.concatenate([latents, noise[:, 0]], axis=0) + after[0]
     planes = to_tokens(with_halo(planes, "dev", 2, 2 * HALO))
     x, noise_wide = planes[0], planes[1:]
     plans = [plan(k) for k in range(STEPS)]

time: 289 us -> 280 us (0.969)
  waiting for transfers between devices: 72.5 us -> 54 us
  local copies, waits for them, and re-layouts: 17.4 us -> 22.1 us
  Pallas kernels: 126 us -> 129 us
    ppermute x14 -> x11, waiting for transfers between devices: 66.3 us -> 34.5 us  [swap(): return lax.ppermute(value, axis, [(i, i ^ mask) for i in range(size)])]
    all_to_all x0 -> x1, waiting for transfers between devices: none -> 13.3 us  [per_device(): lax.all_to_all(wanted, 'sec', split_axis=0, concat_axis=0, tiled=True)]
    ppermute x14 -> x11, starting transfers between devices: 18.9 us -> 13.3 us  [swap(): return lax.ppermute(value, axis, [(i, i ^ mask) for i in range(size)])]
    all_to_all x0 -> x1, starting transfers between devices: none -> 5.07 us  [per_device(): lax.all_to_all(wanted, 'sec', split_axis=0, concat_axis=0, tiled=True)]
    pallas_call x2, Pallas kernels: 126 us -> 129 us  [run_steps(): pl.pallas_call(functools.partial(steps_kernel, rows, cols, counts, split,...]
  transfers between devices with their start and end apart: 20 -> 18, of which waited for: 11 -> 10; matrix products, arithmetic and copies ran while one was open for 7% -> 9% of each run, Pallas kernels for 0% -> 0%
where the time goes in v3:
time: 280 us
  Pallas kernels  129 us (46%)
  waiting for transfers between devices  54 us (19%)
  starting transfers between devices  32.7 us (12%)
  local copies, waits for them, and re-layouts  22.1 us (8%)
  between operations  18.8 us (7%)
  blocking collectives  10.9 us (4%)
  other arithmetic  8.04 us (3%)
  matrix products  3.68 us (1%)
    pallas_call x2, Pallas kernels, run_steps(): pl.pallas_call(functools.partial(steps_kernel, rows, cols, counts, split,...  129 us
    ppermute x11, waiting for transfers between devices, swap(): return lax.ppermute(value, axis, [(i, i ^ mask) for i in range(size)])  34.5 us
    ppermute x11, starting transfers between devices, swap(): return lax.ppermute(value, axis, [(i, i ^ mask) for i in range(size)])  13.3 us
    all_to_all x1, waiting for transfers between devices, per_device(): lax.all_to_all(wanted, 'sec', split_axis=0, concat_axis=0, tiled=True)  13.3 us
    all_to_all x1, blocking collectives, per_device(): lax.all_to_all(block, 'dev', split_axis=0, concat_axis=1, tiled=True)  10.9 us
    all_to_all x1, starting transfers between devices, per_device(): lax.all_to_all(arranged, ('sec', 'dev'), split_axis=0, concat_axis=0, til...  7.96 us
    all_to_all x1, waiting for transfers between devices, per_device(): lax.all_to_all(arranged, ('sec', 'dev'), split_axis=0, concat_axis=0, til...  6.2 us
  transfers between devices with their start and end apart: 18, of which 10 were waited for; matrix products, arithmetic and copies ran while one was open for 9% of the time, Pallas kernels for 0%

profile of v3, /device:TPU:0, one launch (start us, length us, event | category | flops | bytes accessed | tf_op | source)
XLA Modules:
  0.0 279.5 jit_solution(14818498542820117106)
XLA Ops:
  14.0 10.9 %all_to_all.28 = bf16[4,224,160]{1,2,0:T(8,128)(2,1)S(1)} all-to-all(bf16[4,224,160]{1,2,0:T(8,128)(2,1)S(1)} %copy.76), channel_id=1, replica_groups=mesh['sec'=8,'dev'=4] {'dev'}, dimensions={0} | all-to-all | bytes 573440 | tf_op jit(solution)/shard_map/all_to_all | solution.py:462
  28.4 4.3 %collective-permute-done = bf16[1,80,640]{2,1,0:T(8,128)(2,1)S(1)} collective-permute-done((bf16[1,80,640]{2,1,0:T(8,128)(2,1)S(1)}, bf16[1,80,640]{2,1,0:T(8,128)(2,1)S(1)}, u32[]{:S(2)}, u32[]{:S(2)}) %collective-permute-start) | collective-permute-done | bytes 102432 | tf_op jit(solution)/shard_map/ppermute | solution.py:34
  34.0 1.6 collective-permute-start.8
  35.6 1.6 collective-permute-start.1
  37.7 1.6 collective-permute-start.9
  39.3 4.2 %collective-permute-done.9 = f32[2,2]{0,1:T(2,128)S(1)} collective-permute-done((f32[2,2]{0,1:T(2,128)S(1)}, f32[2,2]{0,1:T(2,128)S(1)}, u32[]{:S(2)}, u32[]{:S(2)}) %collective-permute-start.9) | collective-permute-done | bytes 48 | tf_op jit(solution)/shard_map/ppermute | solution.py:34
  43.7 3.2 %collective-permute-start.10 = (f32[4,2]{0,1:T(2,128)S(1)}, f32[4,2]{0,1:T(2,128)S(1)}, u32[]{:S(2)}, u32[]{:S(2)}) collective-permute-start(f32[4,2]{0,1:T(2,128)S(1)} %pad_maximum_fusion.10), channel_id=1, source_target_pairs={{0,16},{4,20},{8,24},{12,28},{16,0},{20,4},{24,8},{28,12},{1,17},{... | collective-permute-start | bytes 104 | tf_op jit(solution)/shard_map/ppermute | solution.py:34
  46.9 1.5 collective-permute-done.10
  51.9 5.1 %all-to-all-start.1 = ((bf16[8,80,320]{2,1,0:T(8,128)(2,1)}), bf16[8,80,320]{2,1,0:T(8,128)(2,1)S(1)}, u32[]{:S(2)}, u32[]{:S(2)}) async-start(bf16[8,80,320]{2,1,0:T(8,128)(2,1)} %copy.82), calls=%async_computation.1 | async-start | bytes 983040 | tf_op jit(solution)/shard_map/all_to_all | solution.py:528
  58.3 1.5 collective-permute-start.7
  60.6 2.9 %collective-permute-start.2 = (bf16[4,80,640]{2,1,0:T(8,128)(2,1)}, bf16[4,80,640]{2,1,0:T(8,128)(2,1)}, u32[]{:S(2)}, u32[]{:S(2)}) collective-permute-start(bf16[4,80,640]{2,1,0:T(8,128)(2,1)} %pad_maximum_fusion.2), channel_id=1, source_target_pairs={{0,16},{4,20},{8,24},{12,28},{16,0},{20,4},{24,8},{28,12},{1,17},{... | collective-permute-start | bytes 1228808 | tf_op jit(solution)/shard_map/ppermute | solution.py:34
  67.6 1.9 reshape.206
  69.5 1.4 copy.110
  70.9 13.3 %all-to-all-done.1 = bf16[8,80,320]{2,1,0:T(8,128)(2,1)S(1)} async-done(((bf16[8,80,320]{2,1,0:T(8,128)(2,1)}), bf16[8,80,320]{2,1,0:T(8,128)(2,1)S(1)}, u32[]{:S(2)}, u32[]{:S(2)}) %all-to-all-start.1) | async-done | bytes 409632 | tf_op jit(solution)/shard_map/all_to_all | solution.py:528
  84.3 16.7 %collective-permute-done.2 = bf16[4,80,640]{2,1,0:T(8,128)(2,1)} collective-permute-done((bf16[4,80,640]{2,1,0:T(8,128)(2,1)}, bf16[4,80,640]{2,1,0:T(8,128)(2,1)}, u32[]{:S(2)}, u32[]{:S(2)}) %collective-permute-start.2) | collective-permute-done | bytes 409632 | tf_op jit(solution)/shard_map/ppermute | solution.py:34
  101.1 2.1 pad_maximum_fusion.refs_1_
  103.1 1.3 collective-permute-start.3
  106.9 3.5 %collective-permute-done.12 = bf16[2,80,320]{2,1,0:T(8,128)(2,1)} collective-permute-done((bf16[2,80,320]{2,1,0:T(8,128)(2,1)}, bf16[2,80,320]{2,1,0:T(8,128)(2,1)}, u32[]{:S(2)}, u32[]{:S(2)}) %collective-permute-start.12) | collective-permute-done | bytes 102432 | tf_op jit(solution)/shard_map/ppermute | solution.py:34
  113.4 3.3 %collective-permute-done.3.refs_2_ = bf16[8,80,640]{2,1,0:T(8,128)(2,1)} collective-permute-done((bf16[8,80,640]{2,1,0:T(8,128)(2,1)}, bf16[8,80,640]{2,1,0:T(8,128)(2,1)}, u32[]{:S(2)}, u32[]{:S(2)}) %collective-permute-start.3) | collective-permute-done | bytes 819232 | tf_op jit(solution)/shard_map/ppermute | solution.py:34
  119.4 64.6 %shard_map.210 = (f32[16,1024]{1,0:T(8,128)S(1)}, f32[16,640]{1,0:T(8,128)S(1)}) custom-call(s32[4]{0:T(128)S(1)} %pad_add_fusion.flags, f32[3,4]{1,0:T(4,128)S(1)} %copy-done.2, bf16[8,576,640]{2,1,0:T(8,128)(2,1)} %bitcast.132, bf16[8,80,640]{2,1,0:T(8,128)(2,1)} %pad_maximum_fusion.refs_1_, bf16[8,80,640]{2,1,0:T(8,128)(2,1)} %collective-permute-done.3.refs_2_, ...), custom_call_target="tpu_custom_call" | custom-call | flops 33973862400 | bytes 9830400 | tf_op jit(solution)/shard_map/pallas_call | solution.py:367
  184.1 2.3 collective-permute-start.13
  190.9 64.7 %shard_map.211 = (f32[16,1024]{1,0:T(8,128)S(1)}, f32[16,640]{1,0:T(8,128)S(1)}) custom-call(s32[4]{0:T(128)S(1)} %pad_add_fusion.flags, f32[3,4]{1,0:T(4,128)S(1)} %copy-done.1, bf16[8,576,640]{2,1,0:T(8,128)(2,1)} %bitcast.133, bf16[8,80,640]{2,1,0:T(8,128)(2,1)} %pad_maximum_fusion.refs_1_, bf16[8,80,640]{2,1,0:T(8,128)(2,1)} %collective-permute-done.3.refs_2_, ...), custom_call_target="tpu_custom_call" | custom-call | flops 33973862400 | bytes 9830400 | tf_op jit(solution)/shard_map/pallas_call | solution.py:367
  256.5 8.0 %all-to-all-start.2 = ((f32[32,1,320]{2,1,0:T(1,128)}), f32[32,1,320]{2,1,0:T(1,128)S(1)}, u32[]{:S(2)}, u32[]{:S(2)}) async-start(f32[32,1,320]{2,1,0:T(1,128)} %all_to_all.24), calls=%async_computation.2 | async-start | bytes 98304 | tf_op jit(solution)/shard_map/all_to_all | solution.py:593
  265.6 6.2 %all-to-all-done.2 = f32[32,1,320]{2,1,0:T(1,128)S(1)} async-done(((f32[32,1,320]{2,1,0:T(1,128)}), f32[32,1,320]{2,1,0:T(1,128)S(1)}, u32[]{:S(2)}, u32[]{:S(2)}) %all-to-all-start.2) | async-done | bytes 40992 | tf_op jit(solution)/shard_map/all_to_all | solution.py:593
  (164 shorter events, 33.0 us)
Async XLA Ops:
  7.2 20.0 %copy-start = (bf16[4,77,2048]{2,0,1:T(4,128)(2,1)S(1)}, bf16[4,77,2048]{2,0,1:T(4,128)(2,1)}, u32[]{:S(2)}) copy-start(bf16[4,77,2048]{2,0,1:T(4,128)(2,1)} %param.23) | copy-start | bytes 3784708
  7.2 109.8 %all-gather.2.cloned.1.call-start = ((), (), s32[]{:S(2)}) async-start(), calls=%async_computation.3 | async-start | bytes 6082560 | tf_op jit(solution)/shard_map/all_gather | solution.py:463
  28.0 4.7 %collective-permute-start = (bf16[1,80,640]{2,1,0:T(8,128)(2,1)S(1)}, bf16[1,80,640]{2,1,0:T(8,128)(2,1)S(1)}, u32[]{:S(2)}, u32[]{:S(2)}) collective-permute-start(bf16[1,80,640]{2,1,0:T(8,128)(2,1)S(1)} %copy.98), channel_id=1, source_target_pairs={{0,2},{1,3},{2,0},{3,1},{4,6},{5,7},{6,4},{7,5},{8,10},{9,11},{10,... | collective-permute-start | bytes 307208 | tf_op jit(solution)/shard_map/ppermute | solution.py:34
  34.0 3.6 %collective-permute-start.8 = (f32[1,2]{0,1:T(2,128)S(1)}, f32[1,2]{0,1:T(2,128)S(1)}, u32[]{:S(2)}, u32[]{:S(2)}) collective-permute-start(f32[1,2]{0,1:T(2,128)S(1)} %maximum_add_fusion.1), channel_id=1, source_target_pairs={{0,4},{4,0},{8,12},{12,8},{16,20},{20,16},{24,28},{28,24},{1,5},{5... | collective-permute-start | bytes 32 | tf_op jit(solution)/shard_map/ppermute | solution.py:34
  35.6 13.0 %collective-permute-start.1 = (bf16[2,80,640]{2,1,0:T(8,128)(2,1)S(1)}, bf16[2,80,640]{2,1,0:T(8,128)(2,1)S(1)}, u32[]{:S(2)}, u32[]{:S(2)}) collective-permute-start(bf16[2,80,640]{2,1,0:T(8,128)(2,1)S(1)} %pad_maximum_fusion.5), channel_id=1, source_target_pairs={{0,8},{4,12},{8,0},{12,4},{16,24},{20,28},{24,16},{28,20},{1,9},{5... | collective-permute-start | bytes 614408 | tf_op jit(solution)/shard_map/ppermute | solution.py:34
  37.7 5.8 %collective-permute-start.9 = (f32[2,2]{0,1:T(2,128)S(1)}, f32[2,2]{0,1:T(2,128)S(1)}, u32[]{:S(2)}, u32[]{:S(2)}) collective-permute-start(f32[2,2]{0,1:T(2,128)S(1)} %pad_maximum_fusion.9), channel_id=1, source_target_pairs={{0,8},{4,12},{8,0},{12,4},{16,24},{20,28},{24,16},{28,20},{1,9},{5... | collective-permute-start | bytes 56 | tf_op jit(solution)/shard_map/ppermute | solution.py:34
  43.7 4.8 %collective-permute-start.10 = (f32[4,2]{0,1:T(2,128)S(1)}, f32[4,2]{0,1:T(2,128)S(1)}, u32[]{:S(2)}, u32[]{:S(2)}) collective-permute-start(f32[4,2]{0,1:T(2,128)S(1)} %pad_maximum_fusion.10), channel_id=1, source_target_pairs={{0,16},{4,20},{8,24},{12,28},{16,0},{20,4},{24,8},{28,12},{1,17},{... | collective-permute-start | bytes 104 | tf_op jit(solution)/shard_map/ppermute | solution.py:34
  48.6 17.6 %copy-start.3 = (bf16[2,80,640]{2,1,0:T(8,128)(2,1)}, bf16[2,80,640]{2,1,0:T(8,128)(2,1)S(1)}, u32[]{:S(2)}) copy-start(bf16[2,80,640]{2,1,0:T(8,128)(2,1)S(1)} %collective-permute-done.1) | copy-start | bytes 614404
  51.9 32.3 %all-to-all-start.1 = ((bf16[8,80,320]{2,1,0:T(8,128)(2,1)}), bf16[8,80,320]{2,1,0:T(8,128)(2,1)S(1)}, u32[]{:S(2)}, u32[]{:S(2)}) async-start(bf16[8,80,320]{2,1,0:T(8,128)(2,1)} %copy.82), calls=%async_computation.1 | async-start | bytes 983040 | tf_op jit(solution)/shard_map/all_to_all | solution.py:528
  57.0 9.3 %collective-permute-start.6 = (f32[7,4,8,128]{3,2,1,0:T(8,128)S(1)}, f32[7,4,8,128]{3,2,1,0:T(8,128)S(1)}, u32[]{:S(2)}, u32[]{:S(2)}) collective-permute-start(f32[7,4,8,128]{3,2,1,0:T(8,128)S(1)} %get-tuple-element.24), channel_id=1, source_target_pairs={{0,1},{1,2},{2,3},{4,5},{5,6},{6,7},{8,9},{9,10},{10,11},{12,13},{... | collective-permute-start | bytes 344072 | tf_op jit(solution)/shard_map/ppermute | solution.py:59
  58.3 8.0 %collective-permute-start.7 = (f32[7,4,8,128]{3,2,1,0:T(8,128)S(1)}, f32[7,4,8,128]{3,2,1,0:T(8,128)}, u32[]{:S(2)}, u32[]{:S(2)}) collective-permute-start(f32[7,4,8,128]{3,2,1,0:T(8,128)S(1)} %get-tuple-element.25), channel_id=1, source_target_pairs={{1,0},{2,1},{3,2},{5,4},{6,5},{7,6},{9,8},{10,9},{11,10},{13,12},{... | collective-permute-start | bytes 344072 | tf_op jit(solution)/shard_map/ppermute | solution.py:60
  60.6 40.5 %collective-permute-start.2 = (bf16[4,80,640]{2,1,0:T(8,128)(2,1)}, bf16[4,80,640]{2,1,0:T(8,128)(2,1)}, u32[]{:S(2)}, u32[]{:S(2)}) collective-permute-start(bf16[4,80,640]{2,1,0:T(8,128)(2,1)} %pad_maximum_fusion.2), channel_id=1, source_target_pairs={{0,16},{4,20},{8,24},{12,28},{16,0},{20,4},{24,8},{28,12},{1,17},{... | collective-permute-start | bytes 1228808 | tf_op jit(solution)/shard_map/ppermute | solution.py:34
  84.3 20.2 %collective-permute-start.11 = (bf16[1,80,320]{2,1,0:T(8,128)(2,1)S(1)}, bf16[1,80,320]{2,1,0:T(8,128)(2,1)S(1)}, u32[]{:S(2)}, u32[]{:S(2)}) collective-permute-start(bf16[1,80,320]{2,1,0:T(8,128)(2,1)S(1)} %bitcast.130), channel_id=1, source_target_pairs={{0,1},{1,0},{2,3},{3,2},{4,5},{5,4},{6,7},{7,6},{8,9},{9,8},{10,11... | collective-permute-start | bytes 153608 | tf_op jit(solution)/shard_map/ppermute | solution.py:34
  103.1 13.6 %collective-permute-start.3 = (bf16[8,80,640]{2,1,0:T(8,128)(2,1)}, bf16[8,80,640]{2,1,0:T(8,128)(2,1)}, u32[]{:S(2)}, u32[]{:S(2)}) collective-permute-start(bf16[8,80,640]{2,1,0:T(8,128)(2,1)} %pad_maximum_fusion.refs_1_), channel_id=1, source_target_pairs={{0,4},{4,0},{8,12},{12,8},{16,20},{20,16},{24,28},{28,24},{1,5},{5... | collective-permute-start | bytes 2457608 | tf_op jit(solution)/shard_map/ppermute | solution.py:34
  105.2 5.2 %collective-permute-start.12 = (bf16[2,80,320]{2,1,0:T(8,128)(2,1)}, bf16[2,80,320]{2,1,0:T(8,128)(2,1)}, u32[]{:S(2)}, u32[]{:S(2)}) collective-permute-start(bf16[2,80,320]{2,1,0:T(8,128)(2,1)} %pad_maximum_fusion.6), channel_id=1, source_target_pairs={{0,2},{1,3},{2,0},{3,1},{4,6},{5,7},{6,4},{7,5},{8,10},{9,11},{10,... | collective-permute-start | bytes 307208 | tf_op jit(solution)/shard_map/ppermute | solution.py:34
  106.8 12.0 %collective-permute-start.4 = (bf16[8,80,640]{2,1,0:T(8,128)(2,1)}, bf16[8,80,640]{2,1,0:T(8,128)(2,1)}, u32[]{:S(2)}, u32[]{:S(2)}) collective-permute-start(bf16[8,80,640]{2,1,0:T(8,128)(2,1)} %pad_maximum_fusion.refs_1_), channel_id=1, source_target_pairs={{0,1},{1,0},{2,3},{3,2},{4,5},{5,4},{6,7},{7,6},{8,9},{9,8},{10,11... | collective-permute-start | bytes 2457608 | tf_op jit(solution)/shard_map/ppermute | solution.py:34
  116.7 2.7 collective-permute-start.5
  119.4 71.5 %copy-start.1 = (f32[3,4]{1,0:T(4,128)S(1)}, f32[3,4]{1,0:T(4,128)}, u32[]{:S(2)}) copy-start(f32[3,4]{1,0:T(4,128)} %constant.109.factors) | copy-start | bytes 148
  184.1 6.8 %collective-permute-start.13 = (f32[16,256]{1,0:T(8,128)S(1)}, f32[16,256]{1,0:T(8,128)S(1)}, u32[]{:S(2)}, u32[]{:S(2)}) collective-permute-start(f32[16,256]{1,0:T(8,128)S(1)} %get-tuple-element.32), channel_id=1, source_target_pairs={{0,1},{1,2},{2,3},{4,5},{5,6},{6,7},{8,9},{9,10},{10,11},{12,13},{... | collective-permute-start | bytes 49160 | tf_op jit(solution)/shard_map/ppermute | solution.py:59
  186.3 4.5 %collective-permute-start.14 = (f32[16,256]{1,0:T(8,128)S(1)}, f32[16,256]{1,0:T(8,128)S(1)}, u32[]{:S(2)}, u32[]{:S(2)}) collective-permute-start(f32[16,256]{1,0:T(8,128)S(1)} %get-tuple-element.33), channel_id=1, source_target_pairs={{1,0},{2,1},{3,2},{5,4},{6,5},{7,6},{9,8},{10,9},{11,10},{13,12},{... | collective-permute-start | bytes 49160 | tf_op jit(solution)/shard_map/ppermute | solution.py:60
  255.6 16.5 %copy-start.13 = (f32[80,4]{0,1:T(4,128)S(1)}, f32[80,4]{0,1:T(4,128)}, u32[]{:S(2)}) copy-start(f32[80,4]{0,1:T(4,128)} %param.34) | copy-start | bytes 3844
  255.6 16.5 %copy-start.17 = (f32[80,4]{0,1:T(4,128)S(1)}, f32[80,4]{0,1:T(4,128)}, u32[]{:S(2)}) copy-start(f32[80,4]{0,1:T(4,128)} %param.35) | copy-start | bytes 3844
  255.6 16.5 %copy-start.18 = (f32[80,4]{0,1:T(4,128)S(1)}, f32[80,4]{0,1:T(4,128)}, u32[]{:S(2)}) copy-start(f32[80,4]{0,1:T(4,128)} %param.36) | copy-start | bytes 3844
  256.5 15.3 %all-to-all-start.2 = ((f32[32,1,320]{2,1,0:T(1,128)}), f32[32,1,320]{2,1,0:T(1,128)S(1)}, u32[]{:S(2)}, u32[]{:S(2)}) async-start(f32[32,1,320]{2,1,0:T(1,128)} %all_to_all.24), calls=%async_computation.2 | async-start | bytes 98304 | tf_op jit(solution)/shard_map/all_to_all | solution.py:593
  (13 other events, 120.0 us)
Sparse Core Ops, SparseCore 0:
  25.8 84.1 all-gather.1

commit v4 on v2

--- a/solution.py
+++ b/solution.py
@@ -46,18 +46,6 @@
             [jnp.where(upper, other, value), jnp.where(upper, value, other)], axis=0
         )
         mask *= 2
-    return value
-
-
-def halved_sum(value, axis, link=jnp.float32):
-    mask = lax.axis_size(axis) // 2
-    while mask >= 1:
-        half = value.shape[0] // 2
-        upper = bit_of(axis, mask)
-        kept = jnp.where(upper, value[half:], value[:half])
-        sent = jnp.where(upper, value[:half], value[half:])
-        value = kept + swap(sent.astype(link), axis, mask).astype(value.dtype)
-        mask //= 2
     return value
 
 
@@ -442,34 +430,13 @@
     unit = 16 * dev_count
     padded = -(-used // unit) * unit
     whole_tiles = all(count % 16 == 0 for count in big)
-    doubled = int(padded * 0.36) // unit * unit if whole_tiles else 0
-    split = counts[0] - doubled
-    pieces = [w_conv[:split]] + pieces[1:]
+    split = counts[0]
     pieces.append(jnp.zeros((padded - used, col_piece), jnp.bfloat16))
-    blocks = [jnp.concatenate(pieces, axis=0), w_conv[split:]]
-    main_length, length = (padded - doubled) // dev_count, doubled // dev_count
-    block = jnp.concatenate([b.reshape(dev_count, -1, col_piece) for b in blocks], axis=1)
-    block = block.reshape(padded, col_piece)
+    block = jnp.concatenate(pieces, axis=0)
     block = lax.all_to_all(block, "dev", split_axis=0, concat_axis=1, tiled=True)
-    packed = lax.all_gather(block[:main_length], ("sec", "dev"), axis=0, tiled=True)
-    packed = packed.reshape(sec_count, padded - doubled, chans)
+    packed = lax.all_gather(block, ("sec", "dev"), axis=0, tiled=True)
+    packed = packed.reshape(sec_count, padded, chans)
     sources, relative = [packed], []
-    if doubled:
-        turns = [("dev", 1 << k) for k in range(1, dev_count.bit_length() - 1)]
-        turns += [("sec", 1 << k) for k in range(1, sec_count.bit_length() - 1)]
-        turns += [("sec", 1), ("dev", 1)]
-        held, places = [block[main_length:][None]], [((0, 0),)]
-        for number, (axis, mask) in enumerate(turns):
-            step = (mask, 0) if axis == "sec" else (0, mask)
-            new = [swap(piece, axis, mask) for piece in held]
-            new_places = [tuple((s ^ step[0], d ^ step[1]) for s, d in p) for p in places]
-            if number < len(turns) - 2:
-                held = [jnp.concatenate(held + new, axis=0)]
-                places = [places[0] + new_places[0]]
-            else:
-                held, places = held + new, places + new_places
-        sources, relative = sources + held, places
-
     at = split + counts[1] + counts[2]
     in_full = packed[:, at : at + counts[3]].reshape(feats, chans)
     at += counts[3]
@@ -512,8 +479,9 @@
     ).reshape(prompt_count, tokens_up, 2 * col_piece)
     wanted = jnp.einsum(
         "ip,ptc->itc", onehot, partial, precision=lax.Precision.HIGHEST
-    )
-    own_part = halved_sum(wanted, "sec", jnp.bfloat16).astype(jnp.bfloat16)
+    ).astype(jnp.bfloat16)
+    arrived = lax.all_to_all(wanted, "sec", split_axis=0, concat_axis=0, tiled=True)
+    own_part = jnp.sum(arrived.astype(jnp.float32), axis=0, keepdims=True).astype(jnp.bfloat16)
     whole = doubled_gather(own_part, "dev").reshape(dev_count, tokens_up, 2, col_piece)
     whole = whole.transpose(2, 1, 0, 3).reshape(2, tokens_up, chans)
     lane = 2 * HEAD

time: 289 us -> 259 us (0.90)
  waiting for transfers between devices: 72.5 us -> 62.7 us
  starting transfers between devices: 30.7 us -> 22.5 us
  other arithmetic: 10.2 us -> 4.8 us
  Pallas kernels: 126 us -> 121 us
    ppermute x14 -> x5, waiting for transfers between devices: 66.3 us -> 8.37 us  [swap(): return lax.ppermute(value, axis, [(i, i ^ mask) for i in range(size)])]
    all_gather x1, waiting for transfers between devices: 0.02 us -> 28.3 us  [per_device(): packed = lax.all_gather(block, ('sec', 'dev'), axis=0, tiled=True)]
    all_to_all x0 -> x1, waiting for transfers between devices: none -> 19.8 us  [per_device(): lax.all_to_all(wanted, 'sec', split_axis=0, concat_axis=0, tiled=True)]
    ppermute x14 -> x5, starting transfers between devices: 18.9 us -> 5.83 us  [swap(): return lax.ppermute(value, axis, [(i, i ^ mask) for i in range(size)])]
    pallas_call x2, Pallas kernels: 126 us -> 121 us  [run_steps(): pl.pallas_call(functools.partial(steps_kernel, rows, cols, counts, split,...]
    all_to_all x0 -> x1, starting transfers between devices: none -> 4.88 us  [per_device(): lax.all_to_all(wanted, 'sec', split_axis=0, concat_axis=0, tiled=True)]
    concatenate x4 -> x0, other arithmetic: 3.21 us -> none  [the longest x3 2.92 us: per_device(): held = [jnp.concatenate(held + new, axis=0)]]
    slice x4 -> x0, local copies, waits for them, and re-layouts: 2.96 us -> none  [the longest x1 1.09 us: per_device(): blocks = [jnp.concatenate(pieces, axis=0), w_conv[split:]]]
  transfers between devices with their start and end apart: 20 -> 12, of which waited for: 11 -> 7; matrix products, arithmetic and copies ran while one was open for 7% -> 5% of each run, Pallas kernels for 0% -> 0%
where the time goes in v4:
time: 259 us; the launch traced here: 258 us
  Pallas kernels  121 us (47%)
  waiting for transfers between devices  62.7 us (24%)
  starting transfers between devices  22.5 us (9%)
  between operations  17.4 us (7%)
  local copies, waits for them, and re-layouts  16.6 us (6%)
  blocking collectives  10.9 us (4%)
  other arithmetic  4.8 us (2%)
    pallas_call x2, Pallas kernels, run_steps(): pl.pallas_call(functools.partial(steps_kernel, rows, cols, counts, split,...  121 us
    all_gather x1, waiting for transfers between devices, per_device(): packed = lax.all_gather(block, ('sec', 'dev'), axis=0, tiled=True)  28.3 us
    all_to_all x1, waiting for transfers between devices, per_device(): lax.all_to_all(wanted, 'sec', split_axis=0, concat_axis=0, tiled=True)  19.8 us
    all_to_all x1, blocking collectives, per_device(): lax.all_to_all(block, 'dev', split_axis=0, concat_axis=1, tiled=True)  10.9 us
    ppermute x5, waiting for transfers between devices, swap(): return lax.ppermute(value, axis, [(i, i ^ mask) for i in range(size)])  8.37 us
    all_to_all x1, waiting for transfers between devices, per_device(): lax.all_to_all(arranged, ('sec', 'dev'), split_axis=0, concat_axis=0, til...  6.2 us
    ppermute x5, starting transfers between devices, swap(): return lax.ppermute(value, axis, [(i, i ^ mask) for i in range(size)])  5.83 us
    all_to_all x1, starting transfers between devices, per_device(): lax.all_to_all(arranged, ('sec', 'dev'), split_axis=0, concat_axis=0, til...  5.36 us
  transfers between devices with their start and end apart: 12, of which 7 were waited for; matrix products, arithmetic and copies ran while one was open for 5% of the time, Pallas kernels for 0%

profile of v4, /device:TPU:0, one launch (start us, length us, event | category | flops | bytes accessed | tf_op | source)
XLA Modules:
  0.0 258.4 jit_solution(5522964020439925556)
XLA Ops:
  8.4 0.9 copy.72
  9.3 0.9 copy.73
  11.0 1.1 concatenate.33
  12.5 10.9 %all_to_all.34 = bf16[4,224,160]{1,2,0:T(8,128)(2,1)S(1)} all-to-all(bf16[4,224,160]{1,2,0:T(8,128)(2,1)S(1)} %copy.76), channel_id=1, replica_groups=mesh['sec'=8,'dev'=4] {'dev'}, dimensions={0} | all-to-all | bytes 573440 | tf_op jit(solution)/shard_map/all_to_all | solution.py:436
  25.6 1.6 collective-permute-start.2
  27.2 1.4 collective-permute-start
  28.6 1.3 collective-permute-start.1
  30.6 1.6 collective-permute-start.3
  32.1 2.0 collective-permute-done.3
  34.3 2.6 %collective-permute-start.4 = (f32[4,2]{0,1:T(2,128)S(1)}, f32[4,2]{0,1:T(2,128)S(1)}, u32[]{:S(2)}, u32[]{:S(2)}) collective-permute-start(f32[4,2]{0,1:T(2,128)S(1)} %pad_maximum_fusion.9), channel_id=1, source_target_pairs={{0,16},{4,20},{8,24},{12,28},{16,0},{20,4},{24,8},{28,12},{1,17},{... | collective-permute-start | bytes 104 | tf_op jit(solution)/shard_map/ppermute | solution.py:33
  36.9 1.9 collective-permute-done.4
  40.5 4.9 %all-to-all-start.1 = ((bf16[8,80,320]{2,1,0:T(8,128)(2,1)}), bf16[8,80,320]{2,1,0:T(8,128)(2,1)S(1)}, u32[]{:S(2)}, u32[]{:S(2)}) async-start(bf16[8,80,320]{2,1,0:T(8,128)(2,1)} %copy.81), calls=%async_computation.1 | async-start | bytes 983040 | tf_op jit(solution)/shard_map/all_to_all | solution.py:483
  47.1 19.8 %all-to-all-done.1 = bf16[8,80,320]{2,1,0:T(8,128)(2,1)S(1)} async-done(((bf16[8,80,320]{2,1,0:T(8,128)(2,1)}), bf16[8,80,320]{2,1,0:T(8,128)(2,1)S(1)}, u32[]{:S(2)}, u32[]{:S(2)}) %all-to-all-start.1) | async-done | bytes 409632 | tf_op jit(solution)/shard_map/all_to_all | solution.py:483
  70.2 0.9 fusion.33
  71.4 4.3 %collective-permute-done.6 = bf16[2,80,320]{2,1,0:T(8,128)(2,1)S(1)} collective-permute-done((bf16[2,80,320]{2,1,0:T(8,128)(2,1)S(1)}, bf16[2,80,320]{2,1,0:T(8,128)(2,1)S(1)}, u32[]{:S(2)}, u32[]{:S(2)}) %collective-permute-start.6) | collective-permute-done | bytes 102432 | tf_op jit(solution)/shard_map/ppermute | solution.py:33
  78.6 28.3 %all-gather.2.cloned.1.call-done = bf16[7168,640]{1,0:T(8,128)(2,1)} async-done(((bf16[224,640]{1,0:T(8,128)(2,1)}), bf16[7168,640]{1,0:T(8,128)(2,1)}) %all-gather.2.cloned.1.call-update) | async-done | bytes 9175056 | tf_op jit(solution)/shard_map/all_gather | solution.py:437
  107.0 1.0 fusion.32
  108.9 60.7 %shard_map.210 = (f32[16,1024]{1,0:T(8,128)S(1)}, f32[16,640]{1,0:T(8,128)S(1)}) custom-call(s32[4]{0:T(128)S(1)} %pad_add_fusion.flags, f32[3,4]{1,0:T(4,128)S(1)} %copy-done.2, bf16[8,896,640]{2,1,0:T(8,128)(2,1)} %bitcast.123, f32[16,1536]{1,0:T(8,128)S(1)} %squeeze.16.refs_1_, f32[3,16,1536]{2,1,0:T(8,128)S(1)} %slice.68.refs_2_, ...), custom_call_target="tpu_custom_call" | custom-call | flops 33973862400 | bytes 9830400 | tf_op jit(solution)/shard_map/pallas_call | solution.py:350
  169.5 2.1 collective-permute-start.7
  171.7 1.5 collective-permute-start.8
  175.2 1.2 slice.78.refs_2_
  176.5 60.6 %shard_map.211 = (f32[16,1024]{1,0:T(8,128)S(1)}, f32[16,640]{1,0:T(8,128)S(1)}) custom-call(s32[4]{0:T(128)S(1)} %pad_add_fusion.flags, f32[3,4]{1,0:T(4,128)S(1)} %copy-done.1, bf16[8,896,640]{2,1,0:T(8,128)(2,1)} %bitcast.124, f32[16,1536]{1,0:T(8,128)S(1)} %pad_maximum_fusion.5.refs_1_, f32[3,16,1536]{2,1,0:T(8,128)S(1)} %slice.78.refs_2_, ...), custom_call_target="tpu_custom_call" | custom-call | flops 33973862400 | bytes 9830400 | tf_op jit(solution)/shard_map/pallas_call | solution.py:350
  238.0 5.4 %all-to-all-start.2 = ((f32[32,1,320]{2,1,0:T(1,128)}), f32[32,1,320]{2,1,0:T(1,128)S(1)}, u32[]{:S(2)}, u32[]{:S(2)}) async-start(f32[32,1,320]{2,1,0:T(1,128)} %all_to_all.30), calls=%async_computation.2 | async-start | bytes 98304 | tf_op jit(solution)/shard_map/all_to_all | solution.py:548
  244.5 6.2 %all-to-all-done.2 = f32[32,1,320]{2,1,0:T(1,128)S(1)} async-done(((f32[32,1,320]{2,1,0:T(1,128)}), f32[32,1,320]{2,1,0:T(1,128)S(1)}, u32[]{:S(2)}, u32[]{:S(2)}) %all-to-all-start.2) | async-done | bytes 40992 | tf_op jit(solution)/shard_map/all_to_all | solution.py:548
  (132 shorter events, 18.0 us)
Async XLA Ops:
  7.2 22.8 %copy-start = (bf16[4,77,2048]{2,0,1:T(4,128)(2,1)S(1)}, bf16[4,77,2048]{2,0,1:T(4,128)(2,1)}, u32[]{:S(2)}) copy-start(bf16[4,77,2048]{2,0,1:T(4,128)(2,1)} %param.23) | copy-start | bytes 3784708
  7.2 99.8 %all-gather.2.cloned.1.call-start = ((), (), s32[]{:S(2)}) async-start(), calls=%async_computation.3 | async-start | bytes 9461760 | tf_op jit(solution)/shard_map/all_gather | solution.py:437
  12.1 15.1 %copy-start.3 = (f32[6,1,4,32,128]{4,3,2,1,0:T(8,128)S(1)}, f32[6,1,4,32,128]{4,3,2,1,0:T(8,128)}, u32[]{:S(2)}) copy-start(f32[6,1,4,32,128]{4,3,2,1,0:T(8,128)} %param.20) | copy-start | bytes 1179652
  12.1 15.1 %copy-start.4 = (f32[1,4,32,128]{3,2,1,0:T(8,128)S(1)}, f32[1,4,32,128]{3,2,1,0:T(8,128)}, u32[]{:S(2)}) copy-start(f32[1,4,32,128]{3,2,1,0:T(8,128)} %param.19) | copy-start | bytes 196612
  12.5 17.6 %copy-start.6 = (bf16[256,160]{0,1:T(8,128)(2,1)S(1)}, bf16[256,160]{0,1:T(8,128)(2,1)}, u32[]{:S(2)}) copy-start(bf16[256,160]{0,1:T(8,128)(2,1)} %param.32) | copy-start | bytes 245764
  12.5 17.6 %copy-start.7 = (bf16[256,160]{0,1:T(8,128)(2,1)S(1)}, bf16[256,160]{0,1:T(8,128)(2,1)}, u32[]{:S(2)}) copy-start(bf16[256,160]{0,1:T(8,128)(2,1)} %param.31) | copy-start | bytes 245764
  25.6 4.8 %collective-permute-start.2 = (f32[1,2]{0,1:T(2,128)S(1)}, f32[1,2]{0,1:T(2,128)S(1)}, u32[]{:S(2)}, u32[]{:S(2)}) collective-permute-start(f32[1,2]{0,1:T(2,128)S(1)} %pad_maximum_fusion.7), channel_id=1, source_target_pairs={{0,4},{4,0},{8,12},{12,8},{16,20},{20,16},{24,28},{28,24},{1,5},{5... | collective-permute-start | bytes 32 | tf_op jit(solution)/shard_map/ppermute | solution.py:33
  27.2 40.4 %collective-permute-start = (f32[7,4,8,128]{3,2,1,0:T(8,128)S(1)}, f32[7,4,8,128]{3,2,1,0:T(8,128)S(1)}, u32[]{:S(2)}, u32[]{:S(2)}) collective-permute-start(f32[7,4,8,128]{3,2,1,0:T(8,128)S(1)} %get-tuple-element.24), channel_id=1, source_target_pairs={{0,1},{1,2},{2,3},{4,5},{5,6},{6,7},{8,9},{9,10},{10,11},{12,13},{... | collective-permute-start | bytes 344072 | tf_op jit(solution)/shard_map/ppermute | solution.py:58
  28.6 39.0 %collective-permute-start.1 = (f32[7,4,8,128]{3,2,1,0:T(8,128)S(1)}, f32[7,4,8,128]{3,2,1,0:T(8,128)S(1)}, u32[]{:S(2)}, u32[]{:S(2)}) collective-permute-start(f32[7,4,8,128]{3,2,1,0:T(8,128)S(1)} %get-tuple-element.25), channel_id=1, source_target_pairs={{1,0},{2,1},{3,2},{5,4},{6,5},{7,6},{9,8},{10,9},{11,10},{13,12},{... | collective-permute-start | bytes 344072 | tf_op jit(solution)/shard_map/ppermute | solution.py:59
  30.6 3.6 %collective-permute-start.3 = (f32[2,2]{0,1:T(2,128)S(1)}, f32[2,2]{0,1:T(2,128)S(1)}, u32[]{:S(2)}, u32[]{:S(2)}) collective-permute-start(f32[2,2]{0,1:T(2,128)S(1)} %pad_maximum_fusion.8), channel_id=1, source_target_pairs={{0,8},{4,12},{8,0},{12,4},{16,24},{20,28},{24,16},{28,20},{1,9},{5... | collective-permute-start | bytes 56 | tf_op jit(solution)/shard_map/ppermute | solution.py:33
  34.3 4.5 %collective-permute-start.4 = (f32[4,2]{0,1:T(2,128)S(1)}, f32[4,2]{0,1:T(2,128)S(1)}, u32[]{:S(2)}, u32[]{:S(2)}) collective-permute-start(f32[4,2]{0,1:T(2,128)S(1)} %pad_maximum_fusion.9), channel_id=1, source_target_pairs={{0,16},{4,20},{8,24},{12,28},{16,0},{20,4},{24,8},{28,12},{1,17},{... | collective-permute-start | bytes 104 | tf_op jit(solution)/shard_map/ppermute | solution.py:33
  38.9 6.6 %copy-start.12 = (f32[640]{0:T(1024)S(1)}, f32[640]{0:T(1024)}, u32[]{:S(2)}) copy-start(f32[640]{0:T(1024)} %param.26) | copy-start | bytes 7684
  38.9 6.6 %copy-start.8 = (f32[6,640]{1,0:T(8,128)S(1)}, f32[6,640]{1,0:T(8,128)}, u32[]{:S(2)}) copy-start(f32[6,640]{1,0:T(8,128)} %param.24) | copy-start | bytes 46084
  40.5 26.3 %all-to-all-start.1 = ((bf16[8,80,320]{2,1,0:T(8,128)(2,1)}), bf16[8,80,320]{2,1,0:T(8,128)(2,1)S(1)}, u32[]{:S(2)}, u32[]{:S(2)}) async-start(bf16[8,80,320]{2,1,0:T(8,128)(2,1)} %copy.81), calls=%async_computation.1 | async-start | bytes 983040 | tf_op jit(solution)/shard_map/all_to_all | solution.py:483
  67.6 1.6 collective-permute-start.5
  70.1 5.6 %collective-permute-start.6 = (bf16[2,80,320]{2,1,0:T(8,128)(2,1)S(1)}, bf16[2,80,320]{2,1,0:T(8,128)(2,1)S(1)}, u32[]{:S(2)}, u32[]{:S(2)}) collective-permute-start(bf16[2,80,320]{2,1,0:T(8,128)(2,1)S(1)} %pad_maximum_fusion.2), channel_id=1, source_target_pairs={{0,2},{1,3},{2,0},{3,1},{4,6},{5,7},{6,4},{7,5},{8,10},{9,11},{10,... | collective-permute-start | bytes 307208 | tf_op jit(solution)/shard_map/ppermute | solution.py:33
  77.9 31.0 %copy-start.2 = (f32[3,4]{1,0:T(4,128)S(1)}, f32[3,4]{1,0:T(4,128)}, u32[]{:S(2)}) copy-start(f32[3,4]{1,0:T(4,128)} %constant.106.factors) | copy-start | bytes 148
  108.8 67.6 %copy-start.1 = (f32[3,4]{1,0:T(4,128)S(1)}, f32[3,4]{1,0:T(4,128)}, u32[]{:S(2)}) copy-start(f32[3,4]{1,0:T(4,128)} %constant.105.factors) | copy-start | bytes 148
  169.5 6.9 %collective-permute-start.7 = (f32[16,256]{1,0:T(8,128)S(1)}, f32[16,256]{1,0:T(8,128)S(1)}, u32[]{:S(2)}, u32[]{:S(2)}) collective-permute-start(f32[16,256]{1,0:T(8,128)S(1)} %get-tuple-element.32), channel_id=1, source_target_pairs={{0,1},{1,2},{2,3},{4,5},{5,6},{6,7},{8,9},{9,10},{10,11},{12,13},{... | collective-permute-start | bytes 49160 | tf_op jit(solution)/shard_map/ppermute | solution.py:58
  171.7 4.7 %collective-permute-start.8 = (f32[16,256]{1,0:T(8,128)S(1)}, f32[16,256]{1,0:T(8,128)S(1)}, u32[]{:S(2)}, u32[]{:S(2)}) collective-permute-start(f32[16,256]{1,0:T(8,128)S(1)} %get-tuple-element.33), channel_id=1, source_target_pairs={{1,0},{2,1},{3,2},{5,4},{6,5},{7,6},{9,8},{10,9},{11,10},{13,12},{... | collective-permute-start | bytes 49160 | tf_op jit(solution)/shard_map/ppermute | solution.py:59
  237.1 13.9 %copy-start.9 = (f32[80,4]{0,1:T(4,128)S(1)}, f32[80,4]{0,1:T(4,128)}, u32[]{:S(2)}) copy-start(f32[80,4]{0,1:T(4,128)} %param.34) | copy-start | bytes 3844
  237.1 13.9 %copy-start.13 = (f32[80,4]{0,1:T(4,128)S(1)}, f32[80,4]{0,1:T(4,128)}, u32[]{:S(2)}) copy-start(f32[80,4]{0,1:T(4,128)} %param.35) | copy-start | bytes 3844
  237.1 13.8 %copy-start.14 = (f32[80,4]{0,1:T(4,128)S(1)}, f32[80,4]{0,1:T(4,128)}, u32[]{:S(2)}) copy-start(f32[80,4]{0,1:T(4,128)} %param.36) | copy-start | bytes 3844
  238.0 12.7 %all-to-all-start.2 = ((f32[32,1,320]{2,1,0:T(1,128)}), f32[32,1,320]{2,1,0:T(1,128)S(1)}, u32[]{:S(2)}, u32[]{:S(2)}) async-start(f32[32,1,320]{2,1,0:T(1,128)} %all_to_all.30), calls=%async_computation.2 | async-start | bytes 98304 | tf_op jit(solution)/shard_map/all_to_all | solution.py:548
  (3 other events, 13.1 us)
Sparse Core Ops, SparseCore 0:
  24.4 82.5 all-gather.1

commit v5 on v4

--- a/solution.py
+++ b/solution.py
@@ -271,7 +271,7 @@
         act = silu_of_twice(rms_scale(output, gains[2:3, :])).astype(jnp.bfloat16)
         predicted = jnp.dot(act, w_final[...], preferred_element_type=jnp.float32)
         span = pl.ds(start, size)
-        noise_now = noise[step, :, span]
+        noise_now = noise[flags[4] + step, :, span]
         state[:, span] = (
             factors[step, 0] * state[:, span]
             + factors[step, 1] * predicted.T
@@ -321,16 +321,19 @@
         def place(number):
             return pl.multiple_of(base + number * size, 2 * cols)
 
-        def rest(number, carry):
-            interleave(
-                finish(step, place(number)), activate(after, place(jnp.maximum(number - 1, 0)))
-            )
+        def beside(number, carry):
+            interleave(finish(step, place(number)), activate(after, place(number - 1)))
             return carry
 
-        lax.fori_loop(0, count, rest, 0)
+        def alone(number, carry):
+            interleave(finish(step, place(number)))
+            return carry
+
+        lax.fori_loop(0, jnp.where(last, count, 1), alone, 0)
 
         @pl.when(step < group - 1)
         def _():
+            lax.fori_loop(1, count, beside, 0)
             interleave(activate(after, place(count - 1)))
 
         return carry
@@ -508,9 +511,7 @@
     )
 
     position = lax.axis_index("dev")
-    flags = jnp.stack(
-        [position > 0, position < dev_count - 1, lax.axis_index("sec"), position]
-    ).astype(jnp.int32)
+    flags = [position > 0, position < dev_count - 1, lax.axis_index("sec"), position]
     planes = jnp.concatenate([latents, noise[:, 0]], axis=0)
     planes = to_tokens(with_halo(planes, "dev", 2, 2 * HALO))
     x, noise_wide = planes[0], planes[1:]
@@ -530,11 +531,11 @@
             big,
             split,
             relative,
-            flags,
+            jnp.stack([jnp.int32(flag) for flag in flags + [first]]),
             factors[part],
             sources,
             x,
-            noise_wide[part],
+            noise_wide,
             rest,
             time_bias[part],
         )

time: 259 us -> 255 us (0.985)
  Pallas kernels: 121 us -> 117 us
    pallas_call x2, Pallas kernels: 121 us -> 117 us  [run_steps(): pl.pallas_call(functools.partial(steps_kernel, rows, cols, counts, split,...]
  transfers between devices with their start and end apart: 12 -> 12, of which waited for: 7 -> 8; matrix products, arithmetic and copies ran while one was open for 5% -> 5% of each run, Pallas kernels for 0% -> 0%
where the time goes in v5:
time: 255 us
  Pallas kernels  117 us (46%)
  waiting for transfers between devices  61.8 us (24%)
  starting transfers between devices  21.6 us (8%)
  local copies, waits for them, and re-layouts  18.5 us (7%)
  between operations  17.3 us (7%)
  blocking collectives  10.9 us (4%)
  other arithmetic  4.86 us (2%)
    pallas_call x2, Pallas kernels, run_steps(): pl.pallas_call(functools.partial(steps_kernel, rows, cols, counts, split,...  117 us
    all_gather x1, waiting for transfers between devices, per_device(): packed = lax.all_gather(block, ('sec', 'dev'), axis=0, tiled=True)  27.7 us
    all_to_all x1, waiting for transfers between devices, per_device(): lax.all_to_all(wanted, 'sec', split_axis=0, concat_axis=0, tiled=True)  18.5 us
    all_to_all x1, blocking collectives, per_device(): lax.all_to_all(block, 'dev', split_axis=0, concat_axis=1, tiled=True)  10.9 us
    ppermute x5, waiting for transfers between devices, swap(): return lax.ppermute(value, axis, [(i, i ^ mask) for i in range(size)])  8.75 us
    all_to_all x1, waiting for transfers between devices, per_device(): lax.all_to_all(arranged, ('sec', 'dev'), split_axis=0, concat_axis=0, til...  6.2 us
    ppermute x5, starting transfers between devices, swap(): return lax.ppermute(value, axis, [(i, i ^ mask) for i in range(size)])  5.83 us
  transfers between devices with their start and end apart: 12, of which 8 were waited for; matrix products, arithmetic and copies ran while one was open for 5% of the time, Pallas kernels for 0%

profile of v5, /device:TPU:0, one launch (start us, length us, event | category | flops | bytes accessed | tf_op | source)
XLA Modules:
  0.0 254.7 jit_solution(16145841171405861496)
XLA Ops:
  11.0 1.1 concatenate.33
  12.5 10.9 %all_to_all.34 = bf16[4,224,160]{1,2,0:T(8,128)(2,1)S(1)} all-to-all(bf16[4,224,160]{1,2,0:T(8,128)(2,1)S(1)} %copy.76), channel_id=1, replica_groups=mesh['sec'=8,'dev'=4] {'dev'}, dimensions={0} | all-to-all | bytes 573440 | tf_op jit(solution)/shard_map/all_to_all | solution.py:439
  25.6 1.6 collective-permute-start.2
  27.2 1.4 collective-permute-start
  28.6 1.3 collective-permute-start.1
  30.5 1.6 collective-permute-start.3
  32.1 2.0 collective-permute-done.3
  34.2 2.6 %collective-permute-start.4 = (f32[4,2]{0,1:T(2,128)S(1)}, f32[4,2]{0,1:T(2,128)S(1)}, u32[]{:S(2)}, u32[]{:S(2)}) collective-permute-start(f32[4,2]{0,1:T(2,128)S(1)} %pad_maximum_fusion.9), channel_id=1, source_target_pairs={{0,16},{4,20},{8,24},{12,28},{16,0},{20,4},{24,8},{28,12},{1,17},{... | collective-permute-start | bytes 104 | tf_op jit(solution)/shard_map/ppermute | solution.py:33
  36.8 1.9 collective-permute-done.4
  40.5 4.9 %all-to-all-start.1 = ((bf16[8,80,320]{2,1,0:T(8,128)(2,1)}), bf16[8,80,320]{2,1,0:T(8,128)(2,1)S(1)}, u32[]{:S(2)}, u32[]{:S(2)}) async-start(bf16[8,80,320]{2,1,0:T(8,128)(2,1)} %copy.81), calls=%async_computation.1 | async-start | bytes 983040 | tf_op jit(solution)/shard_map/all_to_all | solution.py:486
  48.3 18.5 %all-to-all-done.1 = bf16[8,80,320]{2,1,0:T(8,128)(2,1)S(1)} async-done(((bf16[8,80,320]{2,1,0:T(8,128)(2,1)}), bf16[8,80,320]{2,1,0:T(8,128)(2,1)S(1)}, u32[]{:S(2)}, u32[]{:S(2)}) %all-to-all-start.1) | async-done | bytes 409632 | tf_op jit(solution)/shard_map/all_to_all | solution.py:486
  67.1 1.1 collective-permute-done.5
  70.8 3.8 %collective-permute-done.6 = bf16[2,80,320]{2,1,0:T(8,128)(2,1)} collective-permute-done((bf16[2,80,320]{2,1,0:T(8,128)(2,1)}, bf16[2,80,320]{2,1,0:T(8,128)(2,1)}, u32[]{:S(2)}, u32[]{:S(2)}) %collective-permute-start.6) | collective-permute-done | bytes 102432 | tf_op jit(solution)/shard_map/ppermute | solution.py:33
  74.6 1.0 broadcast_select_fusion.2
  77.4 0.9 mul.174
  79.4 27.7 %all-gather.2.cloned.1.call-done = bf16[7168,640]{1,0:T(8,128)(2,1)} async-done(((bf16[224,640]{1,0:T(8,128)(2,1)}), bf16[7168,640]{1,0:T(8,128)(2,1)}) %all-gather.2.cloned.1.call-update) | async-done | bytes 9175056 | tf_op jit(solution)/shard_map/all_gather | solution.py:440
  107.1 1.0 fusion.32
  109.1 1.1 copy.89
  110.5 58.6 %shard_map.210 = (f32[16,1024]{1,0:T(8,128)S(1)}, f32[16,640]{1,0:T(8,128)S(1)}) custom-call(s32[5]{0:T(128)S(1)} %stack.56.flags, f32[3,4]{1,0:T(4,128)S(1)} %copy-done.2, bf16[8,896,640]{2,1,0:T(8,128)(2,1)} %bitcast.122, f32[16,1536]{1,0:T(8,128)S(1)} %squeeze.16.refs_1_, f32[6,16,1536]{2,1,0:T(8,128)S(1)} %slice.58.refs_2_, ...), custom_call_target="tpu_custom_call" | custom-call | flops 33973862400 | bytes 9830400 | tf_op jit(solution)/shard_map/pallas_call | solution.py:353
  169.2 2.2 collective-permute-start.7
  171.4 1.3 collective-permute-start.8
  175.3 58.7 %shard_map.211 = (f32[16,1024]{1,0:T(8,128)S(1)}, f32[16,640]{1,0:T(8,128)S(1)}) custom-call(s32[5]{0:T(128)S(1)} %stack.55.flags, f32[3,4]{1,0:T(4,128)S(1)} %copy-done.1, bf16[8,896,640]{2,1,0:T(8,128)(2,1)} %bitcast.123, f32[16,1536]{1,0:T(8,128)S(1)} %pad_maximum_fusion.5.refs_1_, f32[6,16,1536]{2,1,0:T(8,128)S(1)} %slice.58.refs_2_, ...), custom_call_target="tpu_custom_call" | custom-call | flops 33973862400 | bytes 9830400 | tf_op jit(solution)/shard_map/pallas_call | solution.py:353
  234.9 4.7 %all-to-all-start.2 = ((f32[32,1,320]{2,1,0:T(1,128)}), f32[32,1,320]{2,1,0:T(1,128)S(1)}, u32[]{:S(2)}, u32[]{:S(2)}) async-start(f32[32,1,320]{2,1,0:T(1,128)} %all_to_all.30), calls=%async_computation.2 | async-start | bytes 98304 | tf_op jit(solution)/shard_map/all_to_all | solution.py:549
  240.8 6.2 %all-to-all-done.2 = f32[32,1,320]{2,1,0:T(1,128)S(1)} async-done(((f32[32,1,320]{2,1,0:T(1,128)}), f32[32,1,320]{2,1,0:T(1,128)S(1)}, u32[]{:S(2)}, u32[]{:S(2)}) %all-to-all-start.2) | async-done | bytes 40992 | tf_op jit(solution)/shard_map/all_to_all | solution.py:549
  (138 shorter events, 21.3 us)
Async XLA Ops:
  7.2 22.8 %copy-start = (bf16[4,77,2048]{2,0,1:T(4,128)(2,1)S(1)}, bf16[4,77,2048]{2,0,1:T(4,128)(2,1)}, u32[]{:S(2)}) copy-start(bf16[4,77,2048]{2,0,1:T(4,128)(2,1)} %param.23) | copy-start | bytes 3784708
  7.2 99.9 %all-gather.2.cloned.1.call-start = ((), (), s32[]{:S(2)}) async-start(), calls=%async_computation.3 | async-start | bytes 9461760 | tf_op jit(solution)/shard_map/all_gather | solution.py:440
  12.1 15.1 %copy-start.3 = (f32[6,1,4,32,128]{4,3,2,1,0:T(8,128)S(1)}, f32[6,1,4,32,128]{4,3,2,1,0:T(8,128)}, u32[]{:S(2)}) copy-start(f32[6,1,4,32,128]{4,3,2,1,0:T(8,128)} %param.20) | copy-start | bytes 1179652
  12.1 15.1 %copy-start.6 = (f32[1,4,32,128]{3,2,1,0:T(8,128)S(1)}, f32[1,4,32,128]{3,2,1,0:T(8,128)}, u32[]{:S(2)}) copy-start(f32[1,4,32,128]{3,2,1,0:T(8,128)} %param.19) | copy-start | bytes 196612
  12.5 17.6 %copy-start.9 = (bf16[256,160]{0,1:T(8,128)(2,1)S(1)}, bf16[256,160]{0,1:T(8,128)(2,1)}, u32[]{:S(2)}) copy-start(bf16[256,160]{0,1:T(8,128)(2,1)} %param.32) | copy-start | bytes 245764
  12.5 17.6 %copy-start.10 = (bf16[256,160]{0,1:T(8,128)(2,1)S(1)}, bf16[256,160]{0,1:T(8,128)(2,1)}, u32[]{:S(2)}) copy-start(bf16[256,160]{0,1:T(8,128)(2,1)} %param.31) | copy-start | bytes 245764
  25.6 4.8 %collective-permute-start.2 = (f32[1,2]{0,1:T(2,128)S(1)}, f32[1,2]{0,1:T(2,128)S(1)}, u32[]{:S(2)}, u32[]{:S(2)}) collective-permute-start(f32[1,2]{0,1:T(2,128)S(1)} %pad_maximum_fusion.7), channel_id=1, source_target_pairs={{0,4},{4,0},{8,12},{12,8},{16,20},{20,16},{24,28},{28,24},{1,5},{5... | collective-permute-start | bytes 32 | tf_op jit(solution)/shard_map/ppermute | solution.py:33
  27.2 41.7 %collective-permute-start = (f32[7,4,8,128]{3,2,1,0:T(8,128)S(1)}, f32[7,4,8,128]{3,2,1,0:T(8,128)S(1)}, u32[]{:S(2)}, u32[]{:S(2)}) collective-permute-start(f32[7,4,8,128]{3,2,1,0:T(8,128)S(1)} %get-tuple-element.22), channel_id=1, source_target_pairs={{0,1},{1,2},{2,3},{4,5},{5,6},{6,7},{8,9},{9,10},{10,11},{12,13},{... | collective-permute-start | bytes 344072 | tf_op jit(solution)/shard_map/ppermute | solution.py:58
  28.6 40.3 %collective-permute-start.1 = (f32[7,4,8,128]{3,2,1,0:T(8,128)S(1)}, f32[7,4,8,128]{3,2,1,0:T(8,128)S(1)}, u32[]{:S(2)}, u32[]{:S(2)}) collective-permute-start(f32[7,4,8,128]{3,2,1,0:T(8,128)S(1)} %get-tuple-element.23), channel_id=1, source_target_pairs={{1,0},{2,1},{3,2},{5,4},{6,5},{7,6},{9,8},{10,9},{11,10},{13,12},{... | collective-permute-start | bytes 344072 | tf_op jit(solution)/shard_map/ppermute | solution.py:59
  30.5 3.6 %collective-permute-start.3 = (f32[2,2]{0,1:T(2,128)S(1)}, f32[2,2]{0,1:T(2,128)S(1)}, u32[]{:S(2)}, u32[]{:S(2)}) collective-permute-start(f32[2,2]{0,1:T(2,128)S(1)} %pad_maximum_fusion.8), channel_id=1, source_target_pairs={{0,8},{4,12},{8,0},{12,4},{16,24},{20,28},{24,16},{28,20},{1,9},{5... | collective-permute-start | bytes 56 | tf_op jit(solution)/shard_map/ppermute | solution.py:33
  34.2 4.5 %collective-permute-start.4 = (f32[4,2]{0,1:T(2,128)S(1)}, f32[4,2]{0,1:T(2,128)S(1)}, u32[]{:S(2)}, u32[]{:S(2)}) collective-permute-start(f32[4,2]{0,1:T(2,128)S(1)} %pad_maximum_fusion.9), channel_id=1, source_target_pairs={{0,16},{4,20},{8,24},{12,28},{16,0},{20,4},{24,8},{28,12},{1,17},{... | collective-permute-start | bytes 104 | tf_op jit(solution)/shard_map/ppermute | solution.py:33
  39.7 8.4 %copy-start.15 = (f32[640]{0:T(1024)S(1)}, f32[640]{0:T(1024)}, u32[]{:S(2)}) copy-start(f32[640]{0:T(1024)} %param.26) | copy-start | bytes 7684
  39.7 8.6 %copy-start.11 = (f32[6,640]{1,0:T(8,128)S(1)}, f32[6,640]{1,0:T(8,128)}, u32[]{:S(2)}) copy-start(f32[6,640]{1,0:T(8,128)} %param.24) | copy-start | bytes 46084
  40.5 26.3 %all-to-all-start.1 = ((bf16[8,80,320]{2,1,0:T(8,128)(2,1)}), bf16[8,80,320]{2,1,0:T(8,128)(2,1)S(1)}, u32[]{:S(2)}, u32[]{:S(2)}) async-start(bf16[8,80,320]{2,1,0:T(8,128)(2,1)} %copy.81), calls=%async_computation.1 | async-start | bytes 983040 | tf_op jit(solution)/shard_map/all_to_all | solution.py:486
  66.9 1.3 collective-permute-start.5
  68.9 5.7 %collective-permute-start.6 = (bf16[2,80,320]{2,1,0:T(8,128)(2,1)}, bf16[2,80,320]{2,1,0:T(8,128)(2,1)}, u32[]{:S(2)}, u32[]{:S(2)}) collective-permute-start(bf16[2,80,320]{2,1,0:T(8,128)(2,1)} %pad_maximum_fusion.2), channel_id=1, source_target_pairs={{0,2},{1,3},{2,0},{3,1},{4,6},{5,7},{6,4},{7,5},{8,10},{9,11},{10,... | collective-permute-start | bytes 307208 | tf_op jit(solution)/shard_map/ppermute | solution.py:33
  78.5 32.0 %copy-start.2 = (f32[3,4]{1,0:T(4,128)S(1)}, f32[3,4]{1,0:T(4,128)}, u32[]{:S(2)}) copy-start(f32[3,4]{1,0:T(4,128)} %constant.110.factors) | copy-start | bytes 148
  110.5 64.7 %copy-start.1 = (f32[3,4]{1,0:T(4,128)S(1)}, f32[3,4]{1,0:T(4,128)}, u32[]{:S(2)}) copy-start(f32[3,4]{1,0:T(4,128)} %constant.109.factors) | copy-start | bytes 148
  169.2 5.4 %collective-permute-start.7 = (f32[16,256]{1,0:T(8,128)S(1)}, f32[16,256]{1,0:T(8,128)S(1)}, u32[]{:S(2)}, u32[]{:S(2)}) collective-permute-start(f32[16,256]{1,0:T(8,128)S(1)} %get-tuple-element.30), channel_id=1, source_target_pairs={{0,1},{1,2},{2,3},{4,5},{5,6},{6,7},{8,9},{9,10},{10,11},{12,13},{... | collective-permute-start | bytes 49160 | tf_op jit(solution)/shard_map/ppermute | solution.py:58
  171.4 3.9 %collective-permute-start.8 = (f32[16,256]{1,0:T(8,128)S(1)}, f32[16,256]{1,0:T(8,128)S(1)}, u32[]{:S(2)}, u32[]{:S(2)}) collective-permute-start(f32[16,256]{1,0:T(8,128)S(1)} %get-tuple-element.31), channel_id=1, source_target_pairs={{1,0},{2,1},{3,2},{5,4},{6,5},{7,6},{9,8},{10,9},{11,10},{13,12},{... | collective-permute-start | bytes 49160 | tf_op jit(solution)/shard_map/ppermute | solution.py:59
  234.0 13.2 %copy-start.12 = (f32[80,4]{0,1:T(4,128)S(1)}, f32[80,4]{0,1:T(4,128)}, u32[]{:S(2)}) copy-start(f32[80,4]{0,1:T(4,128)} %param.34) | copy-start | bytes 3844
  234.0 13.2 %copy-start.16 = (f32[80,4]{0,1:T(4,128)S(1)}, f32[80,4]{0,1:T(4,128)}, u32[]{:S(2)}) copy-start(f32[80,4]{0,1:T(4,128)} %param.35) | copy-start | bytes 3844
  234.0 13.2 %copy-start.17 = (f32[80,4]{0,1:T(4,128)S(1)}, f32[80,4]{0,1:T(4,128)}, u32[]{:S(2)}) copy-start(f32[80,4]{0,1:T(4,128)} %param.36) | copy-start | bytes 3844
  234.9 12.1 %all-to-all-start.2 = ((f32[32,1,320]{2,1,0:T(1,128)}), f32[32,1,320]{2,1,0:T(1,128)S(1)}, u32[]{:S(2)}, u32[]{:S(2)}) async-start(f32[32,1,320]{2,1,0:T(1,128)} %all_to_all.30), calls=%async_computation.2 | async-start | bytes 98304 | tf_op jit(solution)/shard_map/all_to_all | solution.py:549
  (6 other events, 19.5 us)
Sparse Core Ops, SparseCore 0:
  24.4 82.5 all-gather.1
